TPU v7x, 32 devices: a whole 2x2x4 slice. The times are simulated.
32 devices in a mesh: blocks: 2 (over y), sec: 8 (over z, x), pln: 2 (over core).
Axes of the slice: x: 2, y: 2, z: 4, core: 2. Of those that a mesh axis runs over, the one named last changes fastest.
Arguments:
- section_tiles: float32 [16, 256, 512], P(('blocks', 'sec'), 'pln'), parts along dimension 0, may hold values from -6 to 6
Outputs:
- flow_scores: float32 [16, 4, 8, 4096], P(('blocks', 'sec'), 'pln'), parts along dimension 0
There are 2 independent parts, one for each index of `blocks`. A program takes and returns all parts, laid end to end along the dimension named above; each array names one. Nothing has to cross between parts.
All inputs are finite; a program needn't handle non-finite values.
Results may differ from a plain program's by a relative error of at most 0.0003.
Values sent between devices are 32-bit elements; how exact they have to be, the bound alone decides.
No kernel may reach another device: no remote copies, remote signals or barrier semaphores. Data moves between devices by JAX's collectives and lax.ppermute only.
A program may use at most 64 MiB of HBM per device.

v0:
```python
import math

import jax
import jax.numpy as jnp
from jax import lax
from jax.sharding import PartitionSpec as P

PATCH = 128
STRIDE = 64
CROP = 64
MARGIN = 32


def from_behind(block, axis, distance):
    devices = range(lax.axis_size(axis))
    route = [(i - distance, i) for i in devices if i - distance in devices]
    return lax.ppermute(block, axis, route)


def padded(array, sides, width):
    for axis, dim in sides:
        devices, length = (lax.axis_size(axis), array.shape[dim])
        up = [(i, (i + 1) % devices) for i in range(devices - 1)]
        down = [(j, i) for i, j in up]
        last = lax.slice_in_dim(array, length - width, length, axis=dim)
        initial = lax.slice_in_dim(array, 0, width, axis=dim)
        before = lax.ppermute(last, axis, up)
        after = lax.ppermute(initial, axis, down)
        array = jnp.concatenate([before, array, after], axis=dim)
    return array


def fourier_tables(count, offset, length):
    first_axis = lax.broadcasted_iota(jnp.int32, (count, length), 0) + offset
    second_axis = lax.broadcasted_iota(jnp.int32, (count, length), 1)
    phase = jnp.mod(first_axis * second_axis, length).astype(jnp.float32) * (2.0 * math.pi / length)
    return (jnp.cos(phase), jnp.sin(phase))


def product(form, left, right):
    return jnp.einsum(
        form, left, right, precision=lax.Precision.HIGHEST, preferred_element_type=jnp.float32
    )


def earlier(field):
    one_back = from_behind(field, "sec", 1)
    two_back = from_behind(field, "sec", 2)
    return (one_back, two_back)


def body(section_tiles):
    section_tile = section_tiles[0]
    bare_one, bare_two = earlier(section_tile)
    stacked = padded(jnp.stack([section_tile, bare_one, bare_two]), (("pln", 1),), MARGIN)
    own_field, one_back, two_back = (stacked[0], stacked[1], stacked[2])
    fields = jnp.stack([own_field, one_back, two_back])
    fields = jnp.pad(fields, ((0, 0), (0, 0), (MARGIN, MARGIN)))
    grid_cols = section_tile.shape[1] // STRIDE
    patch_rows = section_tile.shape[0] // STRIDE
    forward_cos, forward_sin = fourier_tables(PATCH, 0, PATCH)
    inverse_cos, inverse_sin = fourier_tables(CROP, -(CROP // 2), PATCH)
    scale = 1.0 / (PATCH * PATCH * PATCH)

    def split_cols(spectrum_part):
        blocks = spectrum_part.reshape(3, PATCH, grid_cols + 1, STRIDE)
        return jnp.concatenate([blocks[:, :, :-1], blocks[:, :, 1:]], axis=3)

    def one_row(patch_row):
        row_slab = lax.dynamic_slice_in_dim(fields, patch_row * STRIDE, PATCH, 1)
        rows_real = split_cols(product("ka,sab->skb", forward_cos, row_slab))
        rows_imag = split_cols(-product("ka,sab->skb", forward_sin, row_slab))
        spec_real = product("skjb,lb->sjkl", rows_real, forward_cos) + product(
            "skjb,lb->sjkl", rows_imag, forward_sin
        )
        spec_imag = product("skjb,lb->sjkl", rows_imag, forward_cos) - product(
            "skjb,lb->sjkl", rows_real, forward_sin
        )
        own_real, own_imag = (spec_real[0][None], spec_imag[0][None])
        back_real, back_imag = (spec_real[1:], spec_imag[1:])
        cross_real = own_real * back_real + own_imag * back_imag
        cross_imag = own_imag * back_real - own_real * back_imag
        half_real = product("uk,djkl->djul", inverse_cos, cross_real) - product(
            "uk,djkl->djul", inverse_sin, cross_imag
        )
        half_imag = product("uk,djkl->djul", inverse_cos, cross_imag) + product(
            "uk,djkl->djul", inverse_sin, cross_real
        )
        surface = product("djul,vl->djuv", half_real, inverse_cos) - product(
            "djul,vl->djuv", half_imag, inverse_sin
        )
        surface = surface * scale
        joined = surface[0] + surface[1] + surface[0] * surface[1]
        return joined.reshape(grid_cols, CROP * CROP)

    consensus = lax.map(one_row, jnp.arange(patch_rows, dtype=jnp.int32))
    with_rims = padded(consensus, (("pln", 0),), 1)
    rows_mix = with_rims[:-2] + 2.0 * with_rims[1:-1] + with_rims[2:]
    col_padded = jnp.pad(rows_mix, ((0, 0), (1, 1), (0, 0)))
    mixed = (col_padded[:, :-2] + 2.0 * col_padded[:, 1:-1] + col_padded[:, 2:]) / 16.0
    return mixed[None]


def solution(mesh):
    placed = (P(("blocks", "sec"), "pln", None),)
    return jax.shard_map(
        body,
        mesh=mesh,
        in_specs=placed,
        out_specs=P(("blocks", "sec"), "pln", None, None),
        check_vma=False,
    )
```

profile of v0, /device:TPU:11, one launch (start us, length us, event | category | flops | bytes accessed | tf_op | source)
XLA Modules:
  0.0 96.8 jit_solution(4039538151674444254)
XLA Ops:
  0.0 3.2 %collective-permute-start = (f32[128,512]{1,0:T(8,128)}, f32[128,512]{1,0:T(8,128)S(1)}, u32[]{:S(2)}, u32[]{:S(2)}) collective-permute-start(f32[128,512]{1,0:T(8,128)} %bitcast.112), channel_id=1, source_target_pairs={{0,2},{2,4},{4,6},{6,8},{8,10},{10,12},{12,14},{1,3},{3,5},{5,7},{... | collective-permute-start | bytes 786440 | tf_op jit(solution)/shard_map/ppermute | solution.py:17
  3.2 3.2 %collective-permute-start.1 = (f32[128,512]{1,0:T(8,128)}, f32[128,512]{1,0:T(8,128)S(1)}, u32[]{:S(2)}, u32[]{:S(2)}) collective-permute-start(f32[128,512]{1,0:T(8,128)} %bitcast.113), channel_id=1, source_target_pairs={{0,4},{2,6},{4,8},{6,10},{8,12},{10,14},{1,5},{3,7},{5,9},{7,11},{... | collective-permute-start | bytes 786440 | tf_op jit(solution)/shard_map/ppermute | solution.py:17
  6.4 2.9 %collective-permute-done = f32[128,512]{1,0:T(8,128)S(1)} collective-permute-done((f32[128,512]{1,0:T(8,128)}, f32[128,512]{1,0:T(8,128)S(1)}, u32[]{:S(2)}, u32[]{:S(2)}) %collective-permute-start) | collective-permute-done | bytes 262176 | tf_op jit(solution)/shard_map/ppermute | solution.py:17
  9.3 5.6 %collective-permute-done.1 = f32[128,512]{1,0:T(8,128)S(1)} collective-permute-done((f32[128,512]{1,0:T(8,128)}, f32[128,512]{1,0:T(8,128)S(1)}, u32[]{:S(2)}, u32[]{:S(2)}) %collective-permute-start.1) | collective-permute-done | bytes 262176 | tf_op jit(solution)/shard_map/ppermute | solution.py:17
  14.9 0.9 pad_maximum_fusion.11
  15.8 1.3 %collective-permute-start.2 = (f32[3,32,512]{2,1,0:T(8,128)S(1)}, f32[3,32,512]{2,1,0:T(8,128)S(1)}, u32[]{:S(2)}, u32[]{:S(2)}) collective-permute-start(f32[3,32,512]{2,1,0:T(8,128)S(1)} %get-tuple-element.162), channel_id=1, source_target_pairs={{0,1},{2,3},{4,5},{6,7},{8,9},{10,11},{12,13},{14,15},{16,17},{18,... | collective-permute-start | bytes 589832 | tf_op jit(solution)/shard_map/ppermute | solution.py:27
  17.1 3.5 %collective-permute-start.3 = (f32[3,32,512]{2,1,0:T(8,128)S(1)}, f32[3,32,512]{2,1,0:T(8,128)S(1)}, u32[]{:S(2)}, u32[]{:S(2)}) collective-permute-start(f32[3,32,512]{2,1,0:T(8,128)S(1)} %get-tuple-element.163), channel_id=1, source_target_pairs={{1,0},{3,2},{5,4},{7,6},{9,8},{11,10},{13,12},{15,14},{17,16},{19,... | collective-permute-start | bytes 589832 | tf_op jit(solution)/shard_map/ppermute | solution.py:28
  20.6 1.0 %collective-permute-done.3 = f32[3,32,512]{2,1,0:T(8,128)S(1)} collective-permute-done((f32[3,32,512]{2,1,0:T(8,128)S(1)}, f32[3,32,512]{2,1,0:T(8,128)S(1)}, u32[]{:S(2)}, u32[]{:S(2)}) %collective-permute-start.3) | collective-permute-done | bytes 196640 | tf_op jit(solution)/shard_map/ppermute | solution.py:28
  21.6 1.0 %pad_maximum_fusion.6 = f32[3,192,512]{2,1,0:T(8,128)S(1)} fusion(f32[3,32,512]{2,1,0:T(8,128)S(1)} %collective-permute-done.3, f32[1,128,512]{2,1,0:T(8,128)S(1)} %bitcast.117, f32[1,128,512]{2,1,0:T(8,128)S(1)} %bitcast.115, f32[1,128,512]{2,1,0:T(8,128)} %param.3, f32[3,32,512]{2,1,0:T(8,128)S(1)} %collective-permute-done.2), kind=kLoop, calls=%fused_computation.115 | loop fusion | flops 1179648 | bytes 2359296 | tf_op jit(solution)/shard_map/concatenate | solution.py:29
  22.6 0.5 copy.21
  23.1 0.2 pad.8.clone
  23.3 65.3 %while.13 = (s32[]{:T(128)}, f32[2,8,4096]{2,1,0:T(8,128)}, s32[2]{0:T(128)S(1)}, f32[3,192,576]{1,2,0:T(8,128)S(1)}, s32[64]{0:T(128)S(1)}, /*index=5*/s32[]{:T(128)}, s32[1]{0:T(128)}, s32[]{:T(128)}, s32[]{:T(128)}) while((s32[]{:T(128)}, f32[2,8,4096]{2,1,0:T(8,128)}, s32[2]{0:T(128)S(1)}, ...), condition=%wide.region_1.2_spmd.clone.clone.clone, body=%wide.region_0.1_spmd.clone.clone.clone.sunk | while | flops 4110311424 | bytes 71437128 | solution.py:96
  23.3 0.7 dynamic_slice.22
  24.7 1.1 %fusion.167 = f32[3,576,128]{2,1,0:T(8,128)S(1)} fusion(f32[3,192,576]{1,2,0:T(8,128)S(1)} %get-tuple-element.230, s32[]{:T(128)S(6)} %select_n.140), kind=kOutput, calls=%fused_computation.18.clone.1 | convolution fusion | flops 339968000 | bytes 1769476 | tf_op jit(solution)/shard_map/while/body/eval_jaxpr/ka,sab->skb/dot_general | solution.py:41
  25.9 1.1 %fusion.168 = (f32[3,128,8,64]{1,3,2,0:T(8,128)}, f32[3,128,8,64]{1,3,2,0:T(8,128)S(1)}) fusion(f32[3,128,9,64]{1,3,2,0:T(8,128)S(1)} %bitcast.111), kind=kLoop, calls=%fused_computation.130.clone.1 | loop fusion | bytes 3145728 | tf_op jit(solution)/shard_map/while/body/eval_jaxpr/slice | solution.py:67
  26.9 0.5 copy.28
  27.4 1.6 %copy.29 = f32[3,128,8,64]{3,1,2,0:T(8,128)S(1)} copy(f32[3,128,8,64]{1,3,2,0:T(8,128)} %get-tuple-element.206) | data formatting | bytes 1572864 | tf_op jit(solution)/shard_map/while
  29.0 2.8 %fusion.169 = f32[3,128,8,128]{3,1,2,0:T(8,128)} fusion(f32[3,128,8,64]{3,1,2,0:T(8,128)S(1)} %copy.28, f32[3,128,8,64]{3,1,2,0:T(8,128)S(1)} %copy.29), kind=kOutput, calls=%fused_computation.23.clone.1 | convolution fusion | flops 604602368 | bytes 3145728 | tf_op jit(solution)/shard_map/while/body/eval_jaxpr/skjb,lb->sjkl/dot_general | solution.py:41
  31.9 2.6 %convolution_negate_fusion.2 = f32[3,576,128]{2,1,0:T(8,128)S(1)} fusion(f32[3,192,576]{1,2,0:T(8,128)} %copy-done.2, s32[]{:T(128)S(6)} %select_n.140), kind=kOutput, calls=%fused_computation.8.clone.1 | convolution fusion | flops 340189184 | bytes 1769476 | tf_op jit(solution)/shard_map/while/body/eval_jaxpr/ka,sab->skb/dot_general | solution.py:41
  34.5 1.3 %fusion.165 = (f32[3,128,8,64]{1,3,2,0:T(8,128)}, f32[3,128,8,64]{1,3,2,0:T(8,128)}) fusion(f32[3,128,9,64]{1,3,2,0:T(8,128)S(1)} %bitcast.110), kind=kLoop, calls=%fused_computation.131.clone.1 | loop fusion | bytes 3145728 | tf_op jit(solution)/shard_map/while/body/eval_jaxpr/slice | solution.py:67
  35.8 2.8 %copy.26 = f32[3,128,8,64]{3,1,2,0:T(8,128)} copy(f32[3,128,8,64]{1,3,2,0:T(8,128)} %get-tuple-element.203) | data formatting | bytes 1572864 | tf_op jit(solution)/shard_map/while
  38.6 2.8 %copy.27 = f32[3,128,8,64]{3,1,2,0:T(8,128)} copy(f32[3,128,8,64]{1,3,2,0:T(8,128)} %get-tuple-element.204) | data formatting | bytes 1572864 | tf_op jit(solution)/shard_map/while
  41.4 4.3 %add_bitcast_fusion.2 = f32[3,8,128,128]{3,2,1,0:T(8,128)S(1)} fusion(f32[3,128,8,128]{3,1,2,0:T(8,128)} %fusion.169, f32[3,128,8,64]{3,1,2,0:T(8,128)} %copy.26, f32[3,128,8,64]{3,1,2,0:T(8,128)} %copy.27), kind=kOutput, calls=%fused_computation.7.clone.1 | convolution fusion | flops 604995584 | bytes 4718592 | tf_op jit(solution)/shard_map/while/body/eval_jaxpr/skjb,lb->sjkl/dot_general | solution.py:41
  45.7 1.7 %fusion.166 = f32[3,128,8,128]{3,1,2,0:T(8,128)S(1)} fusion(f32[3,128,8,64]{3,1,2,0:T(8,128)S(1)} %copy-done, f32[3,128,8,64]{3,1,2,0:T(8,128)S(1)} %copy-done.1), kind=kOutput, calls=%fused_computation.22.clone.1 | convolution fusion | flops 604602368 | bytes 3145728 | tf_op jit(solution)/shard_map/while/body/eval_jaxpr/skjb,lb->sjkl/dot_general | solution.py:41
  47.5 1.7 %subtract_bitcast_fusion.2 = f32[3,8,128,128]{3,2,1,0:T(8,128)S(1)} fusion(f32[3,128,8,128]{3,1,2,0:T(8,128)S(1)} %fusion.166, f32[3,128,8,64]{3,1,2,0:T(8,128)S(1)} %copy.28, f32[3,128,8,64]{3,1,2,0:T(8,128)S(1)} %copy.29), kind=kOutput, calls=%fused_computation.6.clone.1 | convolution fusion | flops 604995584 | bytes 4718592 | tf_op jit(solution)/shard_map/while/body/eval_jaxpr/skjb,lb->sjkl/dot_general | solution.py:41
  49.2 0.1 slice_bitcast_fusion.3
  49.3 1.0 %fusion.173 = f32[2,8,128,64]{2,3,1,0:T(8,128)S(1)} fusion(s32[64]{0:T(128)S(1)} %get-tuple-element.231, f32[3,8,128,128]{3,2,1,0:T(8,128)S(1)} %subtract_bitcast_fusion.2, f32[3,8,128,128]{3,2,1,0:T(8,128)S(1)} %add_bitcast_fusion.2, f32[8,128,128]{2,1,0:T(8,128)S(1)} %get-tuple-element.207, f32[8,128,128]{2,1,0:T(8,128)S(1)} %get-tuple-element.208), kind=kOutput, calls=%fused_computation.49.clone.1 | convolution fusion | flops 202227712 | bytes 3670528 | tf_op jit(solution)/shard_map/while/body/eval_jaxpr/uk,djkl->djul/dot_general | solution.py:41
  50.4 1.0 %fusion.174 = f32[2,8,64,128]{3,2,1,0:T(8,128)S(1)} fusion(f32[2,8,128,64]{2,3,1,0:T(8,128)S(1)} %fusion.173, s32[64]{0:T(128)S(1)} %get-tuple-element.231, f32[3,8,128,128]{3,2,1,0:T(8,128)S(1)} %subtract_bitcast_fusion.2, f32[3,8,128,128]{3,2,1,0:T(8,128)S(1)} %add_bitcast_fusion.2, f32[8,128,128]{2,1,0:T(8,128)S(1)} %get-tuple-element.207, ...), kind=kOutput, calls=%fused_computation.10.clone.1 | convolution fusion | flops 202358784 | bytes 4194816 | tf_op jit(solution)/shard_map/while/body/eval_jaxpr/uk,djkl->djul/dot_general | solution.py:41
  51.4 1.0 %fusion.170 = f32[2,8,128,64]{2,3,1,0:T(8,128)S(1)} fusion(s32[64]{0:T(128)S(1)} %get-tuple-element.231, f32[3,8,128,128]{3,2,1,0:T(8,128)S(1)} %subtract_bitcast_fusion.2, f32[3,8,128,128]{3,2,1,0:T(8,128)S(1)} %add_bitcast_fusion.2, f32[8,128,128]{2,1,0:T(8,128)S(1)} %get-tuple-element.207, f32[8,128,128]{2,1,0:T(8,128)S(1)} %get-tuple-element.208), kind=kOutput, calls=%fused_computation.53.clone.1 | convolution fusion | flops 202227712 | bytes 3670528 | tf_op jit(solution)/shard_map/while/body/eval_jaxpr/uk,djkl->djul/dot_general | solution.py:41
  52.4 1.0 %fusion.171 = f32[2,8,64,128]{3,2,1,0:T(8,128)S(1)} fusion(f32[2,8,128,64]{2,3,1,0:T(8,128)S(1)} %fusion.170, s32[64]{0:T(128)S(1)} %get-tuple-element.231, f32[3,8,128,128]{3,2,1,0:T(8,128)S(1)} %subtract_bitcast_fusion.2, f32[3,8,128,128]{3,2,1,0:T(8,128)S(1)} %add_bitcast_fusion.2, f32[8,128,128]{2,1,0:T(8,128)S(1)} %get-tuple-element.207, ...), kind=kOutput, calls=%fused_computation.12.clone.1 | convolution fusion | flops 202358784 | bytes 4194816 | tf_op jit(solution)/shard_map/while/body/eval_jaxpr/uk,djkl->djul/dot_general | solution.py:41
  53.5 0.8 fusion.172
  54.3 0.8 fusion.175
  55.1 0.1 add.290
  55.2 0.0 copy-done.4
  55.2 0.7 copy-done.5
  55.9 0.7 dynamic_slice.22
  57.4 1.1 %fusion.167 = f32[3,576,128]{2,1,0:T(8,128)S(1)} fusion(f32[3,192,576]{1,2,0:T(8,128)S(1)} %get-tuple-element.230, s32[]{:T(128)S(6)} %select_n.140), kind=kOutput, calls=%fused_computation.18.clone.1 | convolution fusion | flops 339968000 | bytes 1769476 | tf_op jit(solution)/shard_map/while/body/eval_jaxpr/ka,sab->skb/dot_general | solution.py:41
  58.5 1.1 %fusion.168 = (f32[3,128,8,64]{1,3,2,0:T(8,128)}, f32[3,128,8,64]{1,3,2,0:T(8,128)S(1)}) fusion(f32[3,128,9,64]{1,3,2,0:T(8,128)S(1)} %bitcast.111), kind=kLoop, calls=%fused_computation.130.clone.1 | loop fusion | bytes 3145728 | tf_op jit(solution)/shard_map/while/body/eval_jaxpr/slice | solution.py:67
  59.6 0.5 copy.28
  60.1 1.6 %copy.29 = f32[3,128,8,64]{3,1,2,0:T(8,128)S(1)} copy(f32[3,128,8,64]{1,3,2,0:T(8,128)} %get-tuple-element.206) | data formatting | bytes 1572864 | tf_op jit(solution)/shard_map/while
  61.7 2.8 %fusion.169 = f32[3,128,8,128]{3,1,2,0:T(8,128)} fusion(f32[3,128,8,64]{3,1,2,0:T(8,128)S(1)} %copy.28, f32[3,128,8,64]{3,1,2,0:T(8,128)S(1)} %copy.29), kind=kOutput, calls=%fused_computation.23.clone.1 | convolution fusion | flops 604602368 | bytes 3145728 | tf_op jit(solution)/shard_map/while/body/eval_jaxpr/skjb,lb->sjkl/dot_general | solution.py:41
  64.5 2.6 %convolution_negate_fusion.2 = f32[3,576,128]{2,1,0:T(8,128)S(1)} fusion(f32[3,192,576]{1,2,0:T(8,128)} %copy-done.2, s32[]{:T(128)S(6)} %select_n.140), kind=kOutput, calls=%fused_computation.8.clone.1 | convolution fusion | flops 340189184 | bytes 1769476 | tf_op jit(solution)/shard_map/while/body/eval_jaxpr/ka,sab->skb/dot_general | solution.py:41
  67.1 1.3 %fusion.165 = (f32[3,128,8,64]{1,3,2,0:T(8,128)}, f32[3,128,8,64]{1,3,2,0:T(8,128)}) fusion(f32[3,128,9,64]{1,3,2,0:T(8,128)S(1)} %bitcast.110), kind=kLoop, calls=%fused_computation.131.clone.1 | loop fusion | bytes 3145728 | tf_op jit(solution)/shard_map/while/body/eval_jaxpr/slice | solution.py:67
  68.4 2.8 %copy.26 = f32[3,128,8,64]{3,1,2,0:T(8,128)} copy(f32[3,128,8,64]{1,3,2,0:T(8,128)} %get-tuple-element.203) | data formatting | bytes 1572864 | tf_op jit(solution)/shard_map/while
  71.2 2.8 %copy.27 = f32[3,128,8,64]{3,1,2,0:T(8,128)} copy(f32[3,128,8,64]{1,3,2,0:T(8,128)} %get-tuple-element.204) | data formatting | bytes 1572864 | tf_op jit(solution)/shard_map/while
  74.0 4.3 %add_bitcast_fusion.2 = f32[3,8,128,128]{3,2,1,0:T(8,128)S(1)} fusion(f32[3,128,8,128]{3,1,2,0:T(8,128)} %fusion.169, f32[3,128,8,64]{3,1,2,0:T(8,128)} %copy.26, f32[3,128,8,64]{3,1,2,0:T(8,128)} %copy.27), kind=kOutput, calls=%fused_computation.7.clone.1 | convolution fusion | flops 604995584 | bytes 4718592 | tf_op jit(solution)/shard_map/while/body/eval_jaxpr/skjb,lb->sjkl/dot_general | solution.py:41
  78.4 1.7 %fusion.166 = f32[3,128,8,128]{3,1,2,0:T(8,128)S(1)} fusion(f32[3,128,8,64]{3,1,2,0:T(8,128)S(1)} %copy-done, f32[3,128,8,64]{3,1,2,0:T(8,128)S(1)} %copy-done.1), kind=kOutput, calls=%fused_computation.22.clone.1 | convolution fusion | flops 604602368 | bytes 3145728 | tf_op jit(solution)/shard_map/while/body/eval_jaxpr/skjb,lb->sjkl/dot_general | solution.py:41
  80.1 1.7 %subtract_bitcast_fusion.2 = f32[3,8,128,128]{3,2,1,0:T(8,128)S(1)} fusion(f32[3,128,8,128]{3,1,2,0:T(8,128)S(1)} %fusion.166, f32[3,128,8,64]{3,1,2,0:T(8,128)S(1)} %copy.28, f32[3,128,8,64]{3,1,2,0:T(8,128)S(1)} %copy.29), kind=kOutput, calls=%fused_computation.6.clone.1 | convolution fusion | flops 604995584 | bytes 4718592 | tf_op jit(solution)/shard_map/while/body/eval_jaxpr/skjb,lb->sjkl/dot_general | solution.py:41
  81.9 0.1 slice_bitcast_fusion.3
  82.0 1.0 %fusion.173 = f32[2,8,128,64]{2,3,1,0:T(8,128)S(1)} fusion(s32[64]{0:T(128)S(1)} %get-tuple-element.231, f32[3,8,128,128]{3,2,1,0:T(8,128)S(1)} %subtract_bitcast_fusion.2, f32[3,8,128,128]{3,2,1,0:T(8,128)S(1)} %add_bitcast_fusion.2, f32[8,128,128]{2,1,0:T(8,128)S(1)} %get-tuple-element.207, f32[8,128,128]{2,1,0:T(8,128)S(1)} %get-tuple-element.208), kind=kOutput, calls=%fused_computation.49.clone.1 | convolution fusion | flops 202227712 | bytes 3670528 | tf_op jit(solution)/shard_map/while/body/eval_jaxpr/uk,djkl->djul/dot_general | solution.py:41
  83.0 1.0 %fusion.174 = f32[2,8,64,128]{3,2,1,0:T(8,128)S(1)} fusion(f32[2,8,128,64]{2,3,1,0:T(8,128)S(1)} %fusion.173, s32[64]{0:T(128)S(1)} %get-tuple-element.231, f32[3,8,128,128]{3,2,1,0:T(8,128)S(1)} %subtract_bitcast_fusion.2, f32[3,8,128,128]{3,2,1,0:T(8,128)S(1)} %add_bitcast_fusion.2, f32[8,128,128]{2,1,0:T(8,128)S(1)} %get-tuple-element.207, ...), kind=kOutput, calls=%fused_computation.10.clone.1 | convolution fusion | flops 202358784 | bytes 4194816 | tf_op jit(solution)/shard_map/while/body/eval_jaxpr/uk,djkl->djul/dot_general | solution.py:41
  84.0 1.0 %fusion.170 = f32[2,8,128,64]{2,3,1,0:T(8,128)S(1)} fusion(s32[64]{0:T(128)S(1)} %get-tuple-element.231, f32[3,8,128,128]{3,2,1,0:T(8,128)S(1)} %subtract_bitcast_fusion.2, f32[3,8,128,128]{3,2,1,0:T(8,128)S(1)} %add_bitcast_fusion.2, f32[8,128,128]{2,1,0:T(8,128)S(1)} %get-tuple-element.207, f32[8,128,128]{2,1,0:T(8,128)S(1)} %get-tuple-element.208), kind=kOutput, calls=%fused_computation.53.clone.1 | convolution fusion | flops 202227712 | bytes 3670528 | tf_op jit(solution)/shard_map/while/body/eval_jaxpr/uk,djkl->djul/dot_general | solution.py:41
  85.1 1.0 %fusion.171 = f32[2,8,64,128]{3,2,1,0:T(8,128)S(1)} fusion(f32[2,8,128,64]{2,3,1,0:T(8,128)S(1)} %fusion.170, s32[64]{0:T(128)S(1)} %get-tuple-element.231, f32[3,8,128,128]{3,2,1,0:T(8,128)S(1)} %subtract_bitcast_fusion.2, f32[3,8,128,128]{3,2,1,0:T(8,128)S(1)} %add_bitcast_fusion.2, f32[8,128,128]{2,1,0:T(8,128)S(1)} %get-tuple-element.207, ...), kind=kOutput, calls=%fused_computation.12.clone.1 | convolution fusion | flops 202358784 | bytes 4194816 | tf_op jit(solution)/shard_map/while/body/eval_jaxpr/uk,djkl->djul/dot_general | solution.py:41
  86.1 0.8 fusion.172
  86.9 0.8 fusion.175
  87.7 0.1 add.290
  87.8 0.0 copy-done.4
  87.9 0.7 copy-done.5
  88.6 1.0 %fusion.119 = (f32[1,8,4096]{2,1,0:T(8,128)S(1)}, f32[1,8,4096]{2,1,0:T(8,128)S(1)}) fusion(f32[2,8,4096]{2,1,0:T(8,128)} %get-tuple-element.71), kind=kLoop, calls=%fused_computation.132 | loop fusion | bytes 524288 | tf_op jit(solution)/shard_map/slice | solution.py:25
  89.6 1.3 %collective-permute-start.4 = (f32[1,8,4096]{2,1,0:T(8,128)S(1)}, f32[1,8,4096]{2,1,0:T(8,128)S(1)}, u32[]{:S(2)}, u32[]{:S(2)}) collective-permute-start(f32[1,8,4096]{2,1,0:T(8,128)S(1)} %get-tuple-element.164), channel_id=1, source_target_pairs={{0,1},{2,3},{4,5},{6,7},{8,9},{10,11},{12,13},{14,15},{16,17},{18,... | collective-permute-start | bytes 393224 | tf_op jit(solution)/shard_map/ppermute | solution.py:27
  90.9 3.0 %collective-permute-start.5 = (f32[1,8,4096]{2,1,0:T(8,128)S(1)}, f32[1,8,4096]{2,1,0:T(8,128)S(1)}, u32[]{:S(2)}, u32[]{:S(2)}) collective-permute-start(f32[1,8,4096]{2,1,0:T(8,128)S(1)} %get-tuple-element.165), channel_id=1, source_target_pairs={{1,0},{3,2},{5,4},{7,6},{9,8},{11,10},{13,12},{15,14},{17,16},{19,... | collective-permute-start | bytes 393224 | tf_op jit(solution)/shard_map/ppermute | solution.py:28
  93.9 1.0 collective-permute-done.5
  94.9 1.1 %fusion.115 = f32[2,8,4096]{2,1,0:T(8,128)S(1)} fusion(f32[1,8,4096]{2,1,0:T(8,128)S(1)} %collective-permute-done.5, f32[2,8,4096]{2,1,0:T(8,128)} %get-tuple-element.71, f32[1,8,4096]{2,1,0:T(8,128)S(1)} %collective-permute-done.4), kind=kLoop, calls=%fused_computation.123 | loop fusion | flops 327680 | bytes 786432 | tf_op jit(solution)/shard_map/add | solution.py:98
  96.0 0.8 fusion.114
  (29 shorter events, 0.1 us)
Async XLA Ops:
  0.0 9.3 %collective-permute-start = (f32[128,512]{1,0:T(8,128)}, f32[128,512]{1,0:T(8,128)S(1)}, u32[]{:S(2)}, u32[]{:S(2)}) collective-permute-start(f32[128,512]{1,0:T(8,128)} %bitcast.112), channel_id=1, source_target_pairs={{0,2},{2,4},{4,6},{6,8},{8,10},{10,12},{12,14},{1,3},{3,5},{5,7},{... | collective-permute-start | bytes 786440 | tf_op jit(solution)/shard_map/ppermute | solution.py:17
  3.2 11.7 %collective-permute-start.1 = (f32[128,512]{1,0:T(8,128)}, f32[128,512]{1,0:T(8,128)S(1)}, u32[]{:S(2)}, u32[]{:S(2)}) collective-permute-start(f32[128,512]{1,0:T(8,128)} %bitcast.113), channel_id=1, source_target_pairs={{0,4},{2,6},{4,8},{6,10},{8,12},{10,14},{1,5},{3,7},{5,9},{7,11},{... | collective-permute-start | bytes 786440 | tf_op jit(solution)/shard_map/ppermute | solution.py:17
  15.8 4.8 %collective-permute-start.2 = (f32[3,32,512]{2,1,0:T(8,128)S(1)}, f32[3,32,512]{2,1,0:T(8,128)S(1)}, u32[]{:S(2)}, u32[]{:S(2)}) collective-permute-start(f32[3,32,512]{2,1,0:T(8,128)S(1)} %get-tuple-element.162), channel_id=1, source_target_pairs={{0,1},{2,3},{4,5},{6,7},{8,9},{10,11},{12,13},{14,15},{16,17},{18,... | collective-permute-start | bytes 589832 | tf_op jit(solution)/shard_map/ppermute | solution.py:27
  17.1 4.5 %collective-permute-start.3 = (f32[3,32,512]{2,1,0:T(8,128)S(1)}, f32[3,32,512]{2,1,0:T(8,128)S(1)}, u32[]{:S(2)}, u32[]{:S(2)}) collective-permute-start(f32[3,32,512]{2,1,0:T(8,128)S(1)} %get-tuple-element.163), channel_id=1, source_target_pairs={{1,0},{3,2},{5,4},{7,6},{9,8},{11,10},{13,12},{15,14},{17,16},{19,... | collective-permute-start | bytes 589832 | tf_op jit(solution)/shard_map/ppermute | solution.py:28
  23.3 2.6 %copy-start.2 = (f32[3,192,576]{1,2,0:T(8,128)}, f32[3,192,576]{1,2,0:T(8,128)S(1)}, u32[]{:S(2)}) copy-start(f32[3,192,576]{1,2,0:T(8,128)S(1)} %get-tuple-element.230) | copy-start | bytes 3981316 | tf_op jit(solution)/shard_map/while
  41.4 4.3 %copy-start = (f32[3,128,8,64]{3,1,2,0:T(8,128)S(1)}, f32[3,128,8,64]{3,1,2,0:T(8,128)}, u32[]{:S(2)}) copy-start(f32[3,128,8,64]{3,1,2,0:T(8,128)} %copy.26) | copy-start | bytes 2359300 | tf_op jit(solution)/shard_map/while
  41.4 4.3 %copy-start.1 = (f32[3,128,8,64]{3,1,2,0:T(8,128)S(1)}, f32[3,128,8,64]{3,1,2,0:T(8,128)}, u32[]{:S(2)}) copy-start(f32[3,128,8,64]{3,1,2,0:T(8,128)} %copy.27) | copy-start | bytes 2359300 | tf_op jit(solution)/shard_map/while
  54.3 1.0 copy-start.4
  54.3 1.7 %copy-start.3 = (f32[3,192,576]{1,2,0:T(8,128)S(1)}, f32[3,192,576]{1,2,0:T(8,128)}, u32[]{:S(2)}) copy-start(f32[3,192,576]{1,2,0:T(8,128)} %copy-done.2) | copy-start | bytes 3981316 | tf_op jit(solution)/shard_map/while
  55.2 0.7 copy-start.5
  55.9 2.5 %copy-start.2 = (f32[3,192,576]{1,2,0:T(8,128)}, f32[3,192,576]{1,2,0:T(8,128)S(1)}, u32[]{:S(2)}) copy-start(f32[3,192,576]{1,2,0:T(8,128)S(1)} %get-tuple-element.230) | copy-start | bytes 3981316 | tf_op jit(solution)/shard_map/while
  74.0 4.3 %copy-start = (f32[3,128,8,64]{3,1,2,0:T(8,128)S(1)}, f32[3,128,8,64]{3,1,2,0:T(8,128)}, u32[]{:S(2)}) copy-start(f32[3,128,8,64]{3,1,2,0:T(8,128)} %copy.26) | copy-start | bytes 2359300 | tf_op jit(solution)/shard_map/while
  74.0 4.3 %copy-start.1 = (f32[3,128,8,64]{3,1,2,0:T(8,128)S(1)}, f32[3,128,8,64]{3,1,2,0:T(8,128)}, u32[]{:S(2)}) copy-start(f32[3,128,8,64]{3,1,2,0:T(8,128)} %copy.27) | copy-start | bytes 2359300 | tf_op jit(solution)/shard_map/while
  86.9 1.0 copy-start.4
  86.9 1.7 %copy-start.3 = (f32[3,192,576]{1,2,0:T(8,128)S(1)}, f32[3,192,576]{1,2,0:T(8,128)}, u32[]{:S(2)}) copy-start(f32[3,192,576]{1,2,0:T(8,128)} %copy-done.2) | copy-start | bytes 3981316 | tf_op jit(solution)/shard_map/while
  87.9 0.7 copy-start.5
  89.6 4.4 %collective-permute-start.4 = (f32[1,8,4096]{2,1,0:T(8,128)S(1)}, f32[1,8,4096]{2,1,0:T(8,128)S(1)}, u32[]{:S(2)}, u32[]{:S(2)}) collective-permute-start(f32[1,8,4096]{2,1,0:T(8,128)S(1)} %get-tuple-element.164), channel_id=1, source_target_pairs={{0,1},{2,3},{4,5},{6,7},{8,9},{10,11},{12,13},{14,15},{16,17},{18,... | collective-permute-start | bytes 393224 | tf_op jit(solution)/shard_map/ppermute | solution.py:27
  90.9 4.0 %collective-permute-start.5 = (f32[1,8,4096]{2,1,0:T(8,128)S(1)}, f32[1,8,4096]{2,1,0:T(8,128)S(1)}, u32[]{:S(2)}, u32[]{:S(2)}) collective-permute-start(f32[1,8,4096]{2,1,0:T(8,128)S(1)} %get-tuple-element.165), channel_id=1, source_target_pairs={{1,0},{3,2},{5,4},{7,6},{9,8},{11,10},{13,12},{15,14},{17,16},{19,... | collective-permute-start | bytes 393224 | tf_op jit(solution)/shard_map/ppermute | solution.py:28
where the time goes:
time: 97.5 us; the launch traced here: 96.8 us
  matrix products  39.9 us (41%)
  local copies, waits for them, and re-layouts  25.2 us (26%)
  starting transfers between devices  15.5 us (16%)
  waiting for transfers between devices  10.4 us (11%)
  other arithmetic  3.87 us (4%)
  loops' own time  1.78 us (2%)
    dot_general x24, matrix products, product(): jnp.einsum(form, left, right, precision=lax.Precision.HIGHEST, preferred_...  39.9 us
    while x32, local copies, waits for them, and re-layouts  16.8 us
    ppermute x2, waiting for transfers between devices, from_behind(): return lax.ppermute(block, axis, route)  8.47 us
    ppermute x2, starting transfers between devices, padded(): after = lax.ppermute(initial, axis, down)  6.51 us
    ppermute x2, starting transfers between devices, from_behind(): return lax.ppermute(block, axis, route)  6.37 us
    slice x4, local copies, waits for them, and re-layouts, split_cols(): return jnp.concatenate([blocks[:, :, :-1], blocks[:, :, 1:]], axis=3)  4.86 us
    ppermute x2, starting transfers between devices, padded(): before = lax.ppermute(last, axis, up)  2.58 us
    ppermute x2, waiting for transfers between devices, padded(): after = lax.ppermute(initial, axis, down)  1.96 us
  transfers between devices with their start and end apart: 6, of which 4 were waited for; matrix products, arithmetic and copies ran while one was open for 0% of the time, Pallas kernels for 0%

commit v1 on v0

v1 whole, which is shorter than its diff:
```python
import functools

import jax
import jax.numpy as jnp
import numpy as np
from jax import lax
from jax.experimental import pallas as pl
from jax.experimental.pallas import tpu as pltpu
from jax.sharding import PartitionSpec as P

PATCH = 128
STRIDE = 64
CROP = 64
MARGIN = 32
HALF = PATCH // 2
LANES = 128
PAIRS = CROP // 2
NYQ = 16

BF16 = jnp.bfloat16
F32 = jnp.float32


def high_low(table):
    table = np.asarray(table, np.float32)
    high = table.astype(jnp.bfloat16)
    low = (table - high.astype(np.float32)).astype(jnp.bfloat16)
    return high, low


def tables():
    turn = 2.0 * np.pi / PATCH
    freq, place, full = np.arange(HALF), np.arange(PATCH), np.arange(PATCH)
    angle = turn * (np.outer(freq, place) % PATCH)
    high, low = high_low(np.concatenate([np.cos(angle), -np.sin(angle)]))
    middle = np.tile((-1.0) ** place, (NYQ, 1)).astype(jnp.bfloat16)
    nothing = np.zeros_like(high)
    rows = np.concatenate(
        [np.concatenate([high, high], 1), np.concatenate([middle, middle], 1), np.concatenate([low, nothing], 1)]
    )
    angle = turn * (np.outer(place, full) % PATCH)
    cos, sin = np.cos(angle), np.sin(angle)
    high, low = high_low(np.block([[cos, -sin], [sin, cos]]))
    cols = np.concatenate([high, high, low])
    lags = np.arange(CROP) - CROP // 2
    ordered = np.concatenate([lags[0::2], lags[1::2]])
    weight = np.where(freq == 0, 1.0, 2.0) / PATCH**3
    angle = turn * (np.outer(ordered, freq) % PATCH)
    cos, sin = np.cos(angle) * weight, np.sin(angle) * weight
    high, low = high_low(np.block([[cos, -sin], [sin, cos]]))
    nothing = np.zeros_like(high)
    back_rows = np.block([[high, high], [low, nothing]])
    angle = turn * (np.outer(full, lags) % PATCH)
    one = np.concatenate([np.cos(angle), -np.sin(angle)])
    blank = np.zeros_like(one)
    high, low = high_low(np.block([[one, blank], [blank, one]]))
    back_cols = np.concatenate([high, low], 1)
    return rows, cols, back_rows, back_cols


def dot(left, right):
    return jnp.dot(left, right, preferred_element_type=F32)


def split(value):
    high = value.astype(BF16)
    return high, (value - high.astype(F32)).astype(BF16)


def patch_rows(mine, other, lower):
    edge = MARGIN
    zero = jnp.zeros((edge, mine.shape[1]), F32)
    a0, am, a3 = mine[:edge], mine[edge:-edge], mine[-edge:]
    o0, om, o3 = other[:edge], other[edge:-edge], other[-edge:]
    b0, b3 = jnp.where(lower, a0, o0), jnp.where(lower, o3, a3)
    n0, n3 = jnp.where(lower, zero, a0), jnp.where(lower, a3, zero)
    return [jnp.concatenate(x) for x in ((n0, am, n3), (b0, am, b3), (b0, om, b3))]


def spectrum(pixels, rows, cols, left):
    tiles = pixels.shape[1] // LANES
    patches = pixels.shape[1] // STRIDE
    found = dot(rows, jnp.concatenate(split(pixels)))
    parts = split(found[:PATCH] + found[PATCH + NYQ :])
    middle = found[PATCH : PATCH + 8]
    lane = lax.broadcasted_iota(jnp.int32, (PATCH, LANES), 1)

    def pick(value, j):
        tile = j // 2
        here = value[:, tile * LANES : (tile + 1) * LANES]
        beside = tile + 1 if j % 2 else tile - 1
        if 0 <= beside < tiles:
            there = value[:, beside * LANES : (beside + 1) * LANES]
        else:
            there = jnp.zeros_like(here)
        at = lane[: value.shape[0]]
        return jnp.where(at >= MARGIN if j % 2 else at < LANES - MARGIN, here, there)

    width = 2 * PATCH
    for j in range(patches):
        at = slice(j * HALF, (j + 1) * HALF)
        for base, value in zip((0, width), parts):
            own = pick(value, j)
            left[at, base : base + PATCH] = own[:HALF]
            left[at, base + PATCH : base + width] = own[HALF:]
            if base == 0:
                left[at, 2 * width : 2 * width + PATCH] = own[:HALF]
                left[at, 2 * width + PATCH :] = own[HALF:]
    line = lax.broadcasted_iota(jnp.int32, (8, LANES), 0)
    gathered = jnp.zeros((8, LANES), F32)
    for j in range(patches):
        gathered = jnp.where(line == j, pick(middle, j), gathered)
    high, low = split(jnp.concatenate([gathered, jnp.zeros_like(gathered)]))
    at = slice(patches * HALF, patches * HALF + NYQ)
    blank = jnp.zeros((NYQ, PATCH), BF16)
    for base, value in zip((0, width, 2 * width), (high, low, high)):
        left[at, base : base + PATCH] = value
        left[at, base + PATCH : base + width] = blank
    return dot(left[...], cols[...])


def surface(own, back, back_rows, back_cols, right, lagged):
    patches = (own.shape[0] - NYQ) // HALF
    xr, xi = own[:, :PATCH], own[:, PATCH:]
    yr, yi = back[:, :PATCH], back[:, PATCH:]
    zr, zi = xr * yr + xi * yi, xi * yr - xr * yi
    for j in range(patches):
        at, lanes = slice(j * HALF, (j + 1) * HALF), slice(j * LANES, (j + 1) * LANES)
        for base, value in zip((0, HALF), (zr, zi)):
            high, low = split(value[at])
            right[base : base + HALF, lanes] = high
            right[PATCH + base : PATCH + base + HALF, lanes] = low
    found = dot(back_rows[...], right[...])
    found = found[:PATCH] + found[PATCH:]
    for part in range(2):
        for parity in range(2):
            start = part * CROP + parity * PAIRS
            for j in range(patches):
                block = found[start : start + PAIRS, j * LANES : (j + 1) * LANES]
                lagged[2 * parity + part, pl.ds(j, PAIRS, stride=patches), :] = block
    at = slice(patches * HALF, patches * HALF + patches)
    mr, mi = zr[at] * (1.0 / PATCH**3), zi[at] * (1.0 / PATCH**3)
    value = []
    for q, mid in enumerate((mr, mi, -mr, -mi)):
        plane = lagged[q].reshape(PAIRS, patches, LANES) + mid[None]
        value.append(plane.reshape(PAIRS * patches, LANES))
    value = jnp.concatenate(value, 1)
    found = dot(jnp.concatenate(split(value)), back_cols[...])
    found = found[: PAIRS * patches] + found[PAIRS * patches :]
    return found[:, :LANES] + found[:, LANES:]


def own_kernel(mine, other, rows, cols, out, left):
    lower = lax.axis_index("pln") == 1
    for r, pixels in enumerate(patch_rows(mine[...], other[...], lower)):
        out[r] = spectrum(pixels, rows[...], cols, left.at[r])


def first_kernel(mine, other, own, rows, cols, back_rows, back_cols, out, left, right, lagged):
    lower = lax.axis_index("pln") == 1
    for r, pixels in enumerate(patch_rows(mine[...], other[...], lower)):
        back = spectrum(pixels, rows[...], cols, left.at[r])
        out[r] = surface(own[r], back, back_rows, back_cols, right.at[r], lagged.at[r])


def second_kernel(mine, other, own, first, rows, cols, back_rows, back_cols, out, left, right, lagged):
    pln = lax.axis_index("pln")
    lower = pln == 1
    patches = out.shape[1]
    line = lax.broadcasted_iota(jnp.int32, (PAIRS, patches, LANES), 1)
    mixed = []
    for r, pixels in enumerate(patch_rows(mine[...], other[...], lower)):
        back = spectrum(pixels, rows[...], cols, left.at[r])
        two = surface(own[r], back, back_rows, back_cols, right.at[r], lagged.at[r])
        one = first[r]
        joined = (one + two + one * two).reshape(PAIRS, patches, LANES)
        before = jnp.where(line == 0, 0.0, pltpu.roll(joined, 1, 1))
        after = jnp.where(line == patches - 1, 0.0, pltpu.roll(joined, patches - 1, 1))
        mixed.append((2.0 * joined + before + after) * (1.0 / 16.0))
    outer = 2.0 * mixed[0] + mixed[1]
    inner = mixed[0] + 2.0 * mixed[1] + mixed[2]
    for pair in range(PAIRS):
        lanes = slice(pair * LANES, (pair + 1) * LANES)
        out[pln, :, lanes] = outer[pair]
        out[1 - pln, :, lanes] = inner[pair]


def from_sections(tile, distance, ring):
    count = lax.axis_size("sec")
    route = [(i, (i + distance) % count) for i in range(count) if ring or i + distance < count]
    return lax.ppermute(tile, "sec", route)


def sibling(tile):
    return lax.ppermute(tile, "pln", [(0, 1), (1, 0)])


def body(section_tiles):
    tile = section_tiles[0]
    height, width = tile.shape
    patches = width // STRIDE
    assert height == PATCH and lax.axis_size("pln") == 2 and patches == 8
    rows, cols, back_rows, back_cols = tables()
    packed = patches * HALF + NYQ
    spread = 3
    left = pltpu.VMEM((spread, packed, 6 * PATCH), BF16)
    right = pltpu.VMEM((spread, 2 * PATCH, patches * LANES), BF16)
    lagged = pltpu.VMEM((spread, 4, PAIRS * patches, LANES), F32)
    params = pltpu.CompilerParams(vmem_limit_bytes=48 * 2**20)

    one_back = from_sections(tile, 1, False)
    two_back = from_sections(tile, 2, False)
    own = pl.pallas_call(
        own_kernel,
        out_shape=jax.ShapeDtypeStruct((spread, packed, 2 * PATCH), F32),
        scratch_shapes=[left],
        compiler_params=params,
    )(tile, sibling(tile), rows, cols)
    first = pl.pallas_call(
        first_kernel,
        out_shape=jax.ShapeDtypeStruct((spread, PAIRS * patches, LANES), F32),
        scratch_shapes=[left, right, lagged],
        compiler_params=params,
    )(one_back, sibling(one_back), own, rows, cols, back_rows, back_cols)
    mixed = pl.pallas_call(
        second_kernel,
        out_shape=jax.ShapeDtypeStruct((2, patches, CROP * CROP), F32),
        scratch_shapes=[left, right, lagged],
        compiler_params=params,
    )(two_back, sibling(two_back), own, first, rows, cols, back_rows, back_cols)
    return mixed[None]


def solution(mesh):
    placed = (P(("blocks", "sec"), "pln", None),)
    return jax.shard_map(
        body,
        mesh=mesh,
        in_specs=placed,
        out_specs=P(("blocks", "sec"), "pln", None, None),
        check_vma=False,
    )
```

time: 97.5 us -> 29.7 us (0.30)
  matrix products: 39.9 us -> 0 us
  local copies, waits for them, and re-layouts: 25.2 us -> 2.86 us
  Pallas kernels: 0 us -> 10.1 us
  waiting for transfers between devices: 10.4 us -> 5.31 us
  starting transfers between devices: 15.5 us -> 11.1 us
  other arithmetic: 3.87 us -> 0 us
  loops' own time: 1.78 us -> 0 us
    dot_general x24 -> x0, matrix products: 39.9 us -> none  [product(): jnp.einsum(form, left, right, precision=lax.Precision.HIGHEST, preferred_...]
    while x32 -> x0, local copies, waits for them, and re-layouts: 16.8 us -> none
    pallas_call x0 -> x3, Pallas kernels: none -> 10.1 us  [the longest x1 4.71 us: body(): pl.pallas_call(second_kernel, out_shape=jax.ShapeDtypeStruct((2, patches,...]
    slice x5 -> x0, local copies, waits for them, and re-layouts: 5.84 us -> none  [the longest x4 4.86 us: split_cols(): return jnp.concatenate([blocks[:, :, :-1], blocks[:, :, 1:]], axis=3)]
    ppermute x6 -> x5, waiting for transfers between devices: 10.4 us -> 5.31 us  [the longest x2 5.3 us: from_sections(): return lax.ppermute(tile, 'sec', route)]
    ppermute x6 -> x5, starting transfers between devices: 15.5 us -> 11.1 us  [the longest x2 6.37 us: from_sections(): return lax.ppermute(tile, 'sec', route)]
    unnamed x1 -> x12, local copies, waits for them, and re-layouts: 0.47 us -> 2.86 us
    another operation x1 -> x0, loops' own time: 1.78 us -> none  [body(): consensus = lax.map(one_row, jnp.arange(patch_rows, dtype=jnp.int32))]
  transfers between devices with their start and end apart: 6 -> 5, of which waited for: 4 -> 2; matrix products, arithmetic and copies ran while one was open for 0% -> 0% of each run, Pallas kernels for 0% -> 18%
where the time goes in v1:
time: 29.7 us; the launch traced here: 29.4 us
  starting transfers between devices  11.1 us (37%)
  Pallas kernels  10.1 us (34%)
  waiting for transfers between devices  5.31 us (18%)
  local copies, waits for them, and re-layouts  2.86 us (10%)
    ppermute x2, starting transfers between devices, from_sections(): return lax.ppermute(tile, 'sec', route)  6.37 us
    ppermute x2, waiting for transfers between devices, from_sections(): return lax.ppermute(tile, 'sec', route)  5.3 us
    ppermute x3, starting transfers between devices, sibling(): return lax.ppermute(tile, 'pln', [(0, 1), (1, 0)])  4.71 us
    pallas_call x1, Pallas kernels, body(): pl.pallas_call(second_kernel, out_shape=jax.ShapeDtypeStruct((2, patches,...  4.71 us
    pallas_call x1, Pallas kernels, body(): pl.pallas_call(first_kernel, out_shape=jax.ShapeDtypeStruct((spread, PAIR...  4 us
    unnamed x12, local copies, waits for them, and re-layouts  2.86 us
    pallas_call x1, Pallas kernels, body(): pl.pallas_call(own_kernel, out_shape=jax.ShapeDtypeStruct((spread, packed...  1.4 us
  transfers between devices with their start and end apart: 5, of which 2 were waited for; matrix products, arithmetic and copies ran while one was open for 0% of the time, Pallas kernels for 18%

profile of v1, /device:TPU:11, one launch (start us, length us, event | category | flops | bytes accessed | tf_op | source)
XLA Modules:
  0.0 29.4 jit_solution(7263411934088068601)
XLA Ops:
  0.0 3.2 %collective-permute-start.3 = (f32[128,512]{1,0:T(8,128)}, f32[128,512]{1,0:T(8,128)S(1)}, u32[]{:S(2)}, u32[]{:S(2)}) collective-permute-start(f32[128,512]{1,0:T(8,128)} %bitcast.2), channel_id=1, source_target_pairs={{0,2},{2,4},{4,6},{6,8},{8,10},{10,12},{12,14},{1,3},{3,5},{5,7},{... | collective-permute-start | bytes 786440 | tf_op jit(solution)/shard_map/ppermute | solution.py:191
  3.2 3.2 %collective-permute-start = (f32[128,512]{1,0:T(8,128)}, f32[128,512]{1,0:T(8,128)S(1)}, u32[]{:S(2)}, u32[]{:S(2)}) collective-permute-start(f32[128,512]{1,0:T(8,128)} %bitcast.3), channel_id=1, source_target_pairs={{0,4},{2,6},{4,8},{6,10},{8,12},{10,14},{1,5},{3,7},{5,9},{7,11},{... | collective-permute-start | bytes 786440 | tf_op jit(solution)/shard_map/ppermute | solution.py:191
  6.4 1.3 %collective-permute-start.2 = (f32[128,512]{1,0:T(8,128)}, f32[128,512]{1,0:T(8,128)S(1)}, u32[]{:S(2)}, u32[]{:S(2)}) collective-permute-start(f32[128,512]{1,0:T(8,128)} %bitcast.4), channel_id=1, source_target_pairs={{0,1},{1,0},{2,3},{3,2},{4,5},{5,4},{6,7},{7,6},{8,9},{9,8},{10,11... | collective-permute-start | bytes 786440 | tf_op jit(solution)/shard_map/ppermute | solution.py:195
  7.7 1.6 %collective-permute-done.3.mine = f32[128,512]{1,0:T(8,128)S(1)} collective-permute-done((f32[128,512]{1,0:T(8,128)}, f32[128,512]{1,0:T(8,128)S(1)}, u32[]{:S(2)}, u32[]{:S(2)}) %collective-permute-start.3) | collective-permute-done | bytes 262176 | tf_op jit(solution)/shard_map/ppermute | solution.py:191
  9.3 1.9 %collective-permute-start.4 = (f32[128,512]{1,0:T(8,128)S(1)}, f32[128,512]{1,0:T(8,128)S(1)}, u32[]{:S(2)}, u32[]{:S(2)}) collective-permute-start(f32[128,512]{1,0:T(8,128)S(1)} %collective-permute-done.3.mine), channel_id=1, source_target_pairs={{0,1},{1,0},{2,3},{3,2},{4,5},{5,4},{6,7},{7,6},{8,9},{9,8},{10,11... | collective-permute-start | bytes 786440 | tf_op jit(solution)/shard_map/ppermute | solution.py:195
  11.1 3.7 %collective-permute-done.mine = f32[128,512]{1,0:T(8,128)S(1)} collective-permute-done((f32[128,512]{1,0:T(8,128)}, f32[128,512]{1,0:T(8,128)S(1)}, u32[]{:S(2)}, u32[]{:S(2)}) %collective-permute-start) | collective-permute-done | bytes 262176 | tf_op jit(solution)/shard_map/ppermute | solution.py:191
  14.9 1.5 %collective-permute-start.1 = (f32[128,512]{1,0:T(8,128)S(1)}, f32[128,512]{1,0:T(8,128)S(1)}, u32[]{:S(2)}, u32[]{:S(2)}) collective-permute-start(f32[128,512]{1,0:T(8,128)S(1)} %collective-permute-done.mine), channel_id=1, source_target_pairs={{0,1},{1,0},{2,3},{3,2},{4,5},{5,4},{6,7},{7,6},{8,9},{9,8},{10,11... | collective-permute-start | bytes 786440 | tf_op jit(solution)/shard_map/ppermute | solution.py:195
  16.4 0.0 collective-permute-done.2.other
  16.4 0.0 copy-start
  16.4 1.0 %copy-done = bf16[768,256]{1,0:T(8,128)(2,1)S(1)} copy-done((bf16[768,256]{1,0:T(8,128)(2,1)S(1)}, bf16[768,256]{1,0:T(8,128)(2,1)}, u32[]{:S(2)}) %copy-start) | copy-done | bytes 393240
  17.4 0.0 copy-start.1
  17.4 0.9 %copy-done.1 = bf16[272,256]{1,0:T(8,128)(2,1)S(1)} copy-done((bf16[272,256]{1,0:T(8,128)(2,1)S(1)}, bf16[272,256]{1,0:T(8,128)(2,1)}, u32[]{:S(2)}) %copy-start.1) | copy-done | bytes 139288
  18.3 0.0 copy-start.5
  18.3 0.9 %copy-done.5 = f32[1,128,512]{2,1,0:T(8,128)S(1)} copy-done((f32[1,128,512]{2,1,0:T(8,128)S(1)}, f32[1,128,512]{2,1,0:T(8,128)}, u32[]{:S(2)}) %copy-start.5) | copy-done | bytes 262168
  19.3 0.0 copy-start.2
  19.3 0.0 copy-start.3
  19.3 0.0 copy-start.4
  19.3 1.4 %shard_map.55.own = f32[3,528,256]{2,1,0:T(8,128)S(1)} custom-call(f32[128,512]{1,0:T(8,128)S(1)} %bitcast.5, f32[128,512]{1,0:T(8,128)S(1)} %collective-permute-done.2.other, bf16[272,256]{1,0:T(8,128)(2,1)S(1)} %copy-done.1, bf16[768,256]{1,0:T(8,128)(2,1)S(1)} %copy-done), custom_call_target="tpu_custom_call" | custom-call | tf_op jit(solution)/shard_map/pallas_call | solution.py:213
  20.7 0.0 collective-permute-done.4.other
  20.7 0.0 copy-done.2
  20.7 0.0 copy-done.3
  20.7 0.0 copy-done.4
  20.7 4.0 %shard_map.56.first = f32[3,256,128]{2,1,0:T(8,128)S(1)} custom-call(f32[128,512]{1,0:T(8,128)S(1)} %collective-permute-done.3.mine, f32[128,512]{1,0:T(8,128)S(1)} %collective-permute-done.4.other, f32[3,528,256]{2,1,0:T(8,128)S(1)} %shard_map.55.own, bf16[272,256]{1,0:T(8,128)(2,1)S(1)} %copy-done.2, bf16[768,256]{1,0:T(8,128)(2,1)S(1)} %copy-done, ...), custom_call_target="tpu_custom_call" | custom-call | tf_op jit(solution)/shard_map/pallas_call | solution.py:219
  24.7 0.0 collective-permute-done.1.other
  24.7 4.7 %shard_map.57 = f32[2,8,4096]{2,1,0:T(8,128)} custom-call(f32[128,512]{1,0:T(8,128)S(1)} %collective-permute-done.mine, f32[128,512]{1,0:T(8,128)S(1)} %collective-permute-done.1.other, f32[3,528,256]{2,1,0:T(8,128)S(1)} %shard_map.55.own, f32[3,256,128]{2,1,0:T(8,128)S(1)} %shard_map.56.first, bf16[272,256]{1,0:T(8,128)(2,1)S(1)} %copy-done.2, ...), custom_call_target="tpu_custom_call" | custom-call | tf_op jit(solution)/shard_map/pallas_call | solution.py:225
Async XLA Ops:
  0.0 9.3 %collective-permute-start.3 = (f32[128,512]{1,0:T(8,128)}, f32[128,512]{1,0:T(8,128)S(1)}, u32[]{:S(2)}, u32[]{:S(2)}) collective-permute-start(f32[128,512]{1,0:T(8,128)} %bitcast.2), channel_id=1, source_target_pairs={{0,2},{2,4},{4,6},{6,8},{8,10},{10,12},{12,14},{1,3},{3,5},{5,7},{... | collective-permute-start | bytes 786440 | tf_op jit(solution)/shard_map/ppermute | solution.py:191
  3.2 11.7 %collective-permute-start = (f32[128,512]{1,0:T(8,128)}, f32[128,512]{1,0:T(8,128)S(1)}, u32[]{:S(2)}, u32[]{:S(2)}) collective-permute-start(f32[128,512]{1,0:T(8,128)} %bitcast.3), channel_id=1, source_target_pairs={{0,4},{2,6},{4,8},{6,10},{8,12},{10,14},{1,5},{3,7},{5,9},{7,11},{... | collective-permute-start | bytes 786440 | tf_op jit(solution)/shard_map/ppermute | solution.py:191
  6.4 10.0 %collective-permute-start.2 = (f32[128,512]{1,0:T(8,128)}, f32[128,512]{1,0:T(8,128)S(1)}, u32[]{:S(2)}, u32[]{:S(2)}) collective-permute-start(f32[128,512]{1,0:T(8,128)} %bitcast.4), channel_id=1, source_target_pairs={{0,1},{1,0},{2,3},{3,2},{4,5},{5,4},{6,7},{7,6},{8,9},{9,8},{10,11... | collective-permute-start | bytes 786440 | tf_op jit(solution)/shard_map/ppermute | solution.py:195
  9.3 11.4 %collective-permute-start.4 = (f32[128,512]{1,0:T(8,128)S(1)}, f32[128,512]{1,0:T(8,128)S(1)}, u32[]{:S(2)}, u32[]{:S(2)}) collective-permute-start(f32[128,512]{1,0:T(8,128)S(1)} %collective-permute-done.3.mine), channel_id=1, source_target_pairs={{0,1},{1,0},{2,3},{3,2},{4,5},{5,4},{6,7},{7,6},{8,9},{9,8},{10,11... | collective-permute-start | bytes 786440 | tf_op jit(solution)/shard_map/ppermute | solution.py:195
  14.9 9.9 %collective-permute-start.1 = (f32[128,512]{1,0:T(8,128)S(1)}, f32[128,512]{1,0:T(8,128)S(1)}, u32[]{:S(2)}, u32[]{:S(2)}) collective-permute-start(f32[128,512]{1,0:T(8,128)S(1)} %collective-permute-done.mine), channel_id=1, source_target_pairs={{0,1},{1,0},{2,3},{3,2},{4,5},{5,4},{6,7},{7,6},{8,9},{9,8},{10,11... | collective-permute-start | bytes 786440 | tf_op jit(solution)/shard_map/ppermute | solution.py:195
  16.4 1.0 %copy-start = (bf16[768,256]{1,0:T(8,128)(2,1)S(1)}, bf16[768,256]{1,0:T(8,128)(2,1)}, u32[]{:S(2)}) copy-start(bf16[768,256]{1,0:T(8,128)(2,1)} %constant.9.clone.cols) | copy-start | bytes 1179652
  17.4 0.9 %copy-start.1 = (bf16[272,256]{1,0:T(8,128)(2,1)S(1)}, bf16[272,256]{1,0:T(8,128)(2,1)}, u32[]{:S(2)}) copy-start(bf16[272,256]{1,0:T(8,128)(2,1)} %constant.8.clone.rows) | copy-start | bytes 417796
  18.3 0.9 %copy-start.5 = (f32[1,128,512]{2,1,0:T(8,128)S(1)}, f32[1,128,512]{2,1,0:T(8,128)}, u32[]{:S(2)}) copy-start(f32[1,128,512]{2,1,0:T(8,128)} %param.5) | copy-start | bytes 786436
  19.3 1.4 %copy-start.2 = (bf16[272,256]{1,0:T(8,128)(2,1)S(1)}, bf16[272,256]{1,0:T(8,128)(2,1)}, u32[]{:S(2)}) copy-start(bf16[272,256]{1,0:T(8,128)(2,1)} %constant.8.clone.rows) | copy-start | bytes 417796
  19.3 1.4 %copy-start.3 = (bf16[512,256]{1,0:T(8,128)(2,1)S(1)}, bf16[512,256]{1,0:T(8,128)(2,1)}, u32[]{:S(2)}) copy-start(bf16[512,256]{1,0:T(8,128)(2,1)} %constant.11.clone.back_cols) | copy-start | bytes 786436
  19.3 1.4 %copy-start.4 = (bf16[256,256]{1,0:T(8,128)(2,1)S(1)}, bf16[256,256]{1,0:T(8,128)(2,1)}, u32[]{:S(2)}) copy-start(bf16[256,256]{1,0:T(8,128)(2,1)} %constant.10.clone.back_rows) | copy-start | bytes 393220

commit v2 on v1

v2 whole, which is shorter than its diff:
```python
import functools

import jax
import jax.numpy as jnp
import numpy as np
from jax import lax
from jax.experimental import pallas as pl
from jax.experimental.pallas import tpu as pltpu
from jax.sharding import PartitionSpec as P

PATCH = 128
STRIDE = 64
CROP = 64
MARGIN = 32
HALF = PATCH // 2
LANES = 128
PAIRS = CROP // 2
NYQ = 16

BF16 = jnp.bfloat16
F32 = jnp.float32


def high_low(table):
    table = np.asarray(table, np.float32)
    high = table.astype(jnp.bfloat16)
    low = (table - high.astype(np.float32)).astype(jnp.bfloat16)
    return high, low


def tables():
    turn = 2.0 * np.pi / PATCH
    freq, place, full = np.arange(HALF), np.arange(PATCH), np.arange(PATCH)
    angle = turn * (np.outer(freq, place) % PATCH)
    high, low = high_low(np.concatenate([np.cos(angle), -np.sin(angle)]))
    middle = np.tile((-1.0) ** place, (NYQ, 1)).astype(jnp.bfloat16)
    nothing = np.zeros_like(high)
    rows = np.concatenate(
        [np.concatenate([high, high], 1), np.concatenate([middle, middle], 1), np.concatenate([low, nothing], 1)]
    )
    angle = turn * (np.outer(place, full) % PATCH)
    cos, sin = np.cos(angle), np.sin(angle)
    high, low = high_low(np.block([[cos, -sin], [sin, cos]]))
    cols = np.concatenate([high, high, low])
    lags = np.arange(CROP) - CROP // 2
    angle = turn * (np.outer(full, lags) % PATCH)
    cos, sin = np.cos(angle), np.sin(angle)
    high, low = high_low(np.block([[cos, sin], [-sin, cos]]))
    back_cols = np.concatenate([high, low], 1)
    ordered = np.concatenate([lags[0::2], lags[1::2]])
    weight = np.where(freq == 0, 1.0, 2.0) / PATCH**3
    angle = turn * (np.outer(ordered, freq) % PATCH)
    high, low = high_low(np.concatenate([np.cos(angle) * weight, -np.sin(angle) * weight]))
    back_rows = np.concatenate([high, high, low], 1)
    return rows, cols, back_rows, back_cols


def dot(left, right):
    return jnp.dot(left, right, preferred_element_type=F32)


def split(value):
    high = value.astype(BF16)
    return high, (value - high.astype(F32)).astype(BF16)


def outer_row(mine, lower):
    zero = jnp.zeros((MARGIN, mine.shape[1]), F32)
    first, last = mine[:MARGIN], mine[-MARGIN:]
    return jnp.concatenate([jnp.where(lower, zero, first), mine[MARGIN:-MARGIN], jnp.where(lower, last, zero)])


def inner_rows(mine, other, lower):
    first = jnp.where(lower, mine[:MARGIN], other[:MARGIN])
    last = jnp.where(lower, other[-MARGIN:], mine[-MARGIN:])
    return [jnp.concatenate([first, x[MARGIN:-MARGIN], last]) for x in (mine, other)]


def spectrum(pixels, rows, cols, left):
    tiles = pixels.shape[1] // LANES
    patches = pixels.shape[1] // STRIDE
    found = dot(rows, jnp.concatenate(split(pixels)))
    parts = split(found[:PATCH] + found[PATCH + NYQ :])
    middle = found[PATCH : PATCH + 8]
    lane = lax.broadcasted_iota(jnp.int32, (PATCH, LANES), 1)

    def pick(value, j):
        tile = j // 2
        here = value[:, tile * LANES : (tile + 1) * LANES]
        beside = tile + 1 if j % 2 else tile - 1
        if 0 <= beside < tiles:
            there = value[:, beside * LANES : (beside + 1) * LANES]
        else:
            there = jnp.zeros_like(here)
        at = lane[: value.shape[0]]
        return jnp.where(at >= MARGIN if j % 2 else at < LANES - MARGIN, here, there)

    width = 2 * PATCH
    for j in range(patches):
        at = slice(j * HALF, (j + 1) * HALF)
        for base, value in zip((0, width), parts):
            own = pick(value, j)
            left[at, base : base + PATCH] = own[:HALF]
            left[at, base + PATCH : base + width] = own[HALF:]
            if base == 0:
                left[at, 2 * width : 2 * width + PATCH] = own[:HALF]
                left[at, 2 * width + PATCH :] = own[HALF:]
    line = lax.broadcasted_iota(jnp.int32, (8, LANES), 0)
    gathered = jnp.zeros((8, LANES), F32)
    for j in range(patches):
        gathered = jnp.where(line == j, pick(middle, j), gathered)
    high, low = split(jnp.concatenate([gathered, jnp.zeros_like(gathered)]))
    at = slice(patches * HALF, patches * HALF + NYQ)
    blank = jnp.zeros((NYQ, PATCH), BF16)
    for base, value in zip((0, width, 2 * width), (high, low, high)):
        left[at, base : base + PATCH] = value
        left[at, base + PATCH : base + width] = blank
    return dot(left[...], cols[...])


def surface(own, back, back_rows, back_cols, right, lagged):
    patches = (own.shape[0] - NYQ) // HALF
    xr, xi = own[:, :PATCH], own[:, PATCH:]
    yr, yi = back[:, :PATCH], back[:, PATCH:]
    product = jnp.concatenate([xr * yr + xi * yi, xi * yr - xr * yi], 1)
    found = dot(jnp.concatenate(split(product)), back_cols[...])
    size = own.shape[0]
    found = (found[:size, :LANES] + found[size:, :LANES]) + (found[:size, LANES:] + found[size:, LANES:])
    high, low = split(found[: patches * HALF])
    for j in range(patches):
        at, lanes = slice(j * HALF, (j + 1) * HALF), slice(j * LANES, (j + 1) * LANES)
        right[:HALF, lanes] = high[at]
        right[HALF : 2 * HALF, lanes] = low[at]
        right[2 * HALF :, lanes] = high[at]
    middle = found[patches * HALF : patches * HALF + patches] * (1.0 / PATCH**3)
    found = dot(back_rows[...], right[...])
    lane = lax.broadcasted_iota(jnp.int32, (PAIRS, LANES), 1)
    for j in range(patches):
        lanes = slice(j * LANES, (j + 1) * LANES)
        cos_even, cos_odd, sin_even, sin_odd = (found[q * PAIRS : (q + 1) * PAIRS, lanes] for q in range(4))
        stay = jnp.where(lane < CROP, cos_even, sin_odd)
        move = jnp.where(lane < CROP, cos_odd, sin_even)
        lagged[pl.ds(j, PAIRS, stride=patches), :] = stay + pltpu.roll(move, CROP, 1)
    middle = jnp.where(lane[:patches] < CROP, middle, -pltpu.roll(middle, CROP, 1))
    return lagged[...].reshape(PAIRS, patches, LANES) + middle[None]


def own_kernel(mine, other, rows, cols, out, left):
    lower = lax.axis_index("pln") == 1
    mine, other = mine[...], other[...]
    for r, pixels in enumerate([outer_row(mine, lower)] + inner_rows(mine, other, lower)):
        out[r] = spectrum(pixels, rows[...], cols, left.at[r])


def first_kernel(mine, other, own, rows, cols, back_rows, back_cols, out, left, right, lagged):
    lower = lax.axis_index("pln") == 1
    mine, other = mine[...], other[1 - lax.axis_index("pln")]
    for r, pixels in enumerate([outer_row(mine, lower)] + inner_rows(mine, other, lower)):
        back = spectrum(pixels, rows[...], cols, left.at[r])
        out[r] = surface(own[r], back, back_rows, back_cols, right.at[r], lagged.at[r])


def joined_row(one, two):
    joined = one + two + one * two
    patches = joined.shape[1]
    line = lax.broadcasted_iota(jnp.int32, joined.shape, 1)
    before = jnp.where(line == 0, 0.0, pltpu.roll(joined, 1, 1))
    after = jnp.where(line == patches - 1, 0.0, pltpu.roll(joined, patches - 1, 1))
    return (2.0 * joined + before + after) * (1.0 / 16.0)


def outer_kernel(mine, own, first, rows, cols, back_rows, back_cols, out, left, right, lagged):
    lower = lax.axis_index("pln") == 1
    back = spectrum(outer_row(mine[...], lower), rows[...], cols, left)
    out[...] = joined_row(first[0], surface(own[0], back, back_rows, back_cols, right, lagged))


def inner_kernel(mine, other, own, first, outer, rows, cols, back_rows, back_cols, out, left, right, lagged):
    pln = lax.axis_index("pln")
    mixed = []
    for r, pixels in enumerate(inner_rows(mine[...], other[...], pln == 1)):
        back = spectrum(pixels, rows[...], cols, left.at[r])
        two = surface(own[r + 1], back, back_rows, back_cols, right.at[r], lagged.at[r])
        mixed.append(joined_row(first[r + 1], two))
    ending = outer[...]
    ends = 2.0 * ending + mixed[0]
    inside = ending + 2.0 * mixed[0] + mixed[1]
    for pair in range(PAIRS):
        lanes = slice(pair * LANES, (pair + 1) * LANES)
        out[pln, :, lanes] = ends[pair]
        out[1 - pln, :, lanes] = inside[pair]


def from_sections(tile, distance, ring):
    count = lax.axis_size("sec")
    route = [(i, (i + distance) % count) for i in range(count) if ring or i + distance < count]
    return lax.ppermute(tile, "sec", route)


def sibling(tile):
    return lax.ppermute(tile, "pln", [(0, 1), (1, 0)])


def body(section_tiles):
    tile = section_tiles[0]
    height, width = tile.shape
    patches = width // STRIDE
    assert height == PATCH and lax.axis_size("pln") == 2 and patches == 8
    rows, cols, back_rows, back_cols = tables()
    packed = patches * HALF + NYQ
    surfaces = (PAIRS, patches, LANES)

    def call(kernel, shape, spread, micros, *args):
        scratch = [
            pltpu.VMEM(spread + (packed, 6 * PATCH), BF16),
            pltpu.VMEM(spread + (3 * HALF, patches * LANES), BF16),
            pltpu.VMEM(spread + (PAIRS * patches, LANES), F32),
        ]
        return pl.pallas_call(
            kernel,
            out_shape=jax.ShapeDtypeStruct(shape, F32),
            scratch_shapes=scratch[:1] if kernel is own_kernel else scratch,
            cost_estimate=pl.CostEstimate(flops=int(micros * 1e7), bytes_accessed=int(micros * 3e4), transcendentals=0),
            compiler_params=pltpu.CompilerParams(vmem_limit_bytes=48 * 2**20),
        )(*args)

    one_back = from_sections(tile, 1, False)
    two_back = from_sections(tile, 2, False)
    own = call(own_kernel, (3, packed, 2 * PATCH), (3,), 1.4, tile, sibling(tile), rows, cols)
    one_back, own = lax.optimization_barrier((one_back, own))
    first = call(first_kernel, (3,) + surfaces, (3,), 3.6, one_back, lax.all_gather(one_back, 'pln'), own, rows, cols, back_rows, back_cols)
    two_back, first = lax.optimization_barrier((two_back, first))
    other = sibling(two_back)
    outer = call(outer_kernel, surfaces, (), 1.5, two_back, own, first, rows, cols, back_rows, back_cols)
    mixed = call(
        inner_kernel, (2, patches, CROP * CROP), (2,), 3.0, two_back, other, own, first, outer, rows, cols, back_rows, back_cols
    )
    return mixed[None]


def solution(mesh):
    placed = (P(("blocks", "sec"), "pln", None),)
    return jax.shard_map(
        body,
        mesh=mesh,
        in_specs=placed,
        out_specs=P(("blocks", "sec"), "pln", None, None),
        check_vma=False,
    )
```

time: 29.7 us -> 23.7 us (0.80)
  the two profiles are of different devices: /device:TPU:11 before, /device:TPU:0 now
where the time goes in v2:
time: 23.7 us; the launch traced here: 23.5 us
  Pallas kernels  9.82 us (41%)
  starting transfers between devices  8.53 us (36%)
  local copies, waits for them, and re-layouts  2.86 us (12%)
  blocking collectives  2.18 us (9%)
    pallas_call x4, Pallas kernels, call(): pl.pallas_call(kernel, out_shape=jax.ShapeDtypeStruct(shape, F32), scratc...  9.82 us
    ppermute x2, starting transfers between devices, from_sections(): return lax.ppermute(tile, 'sec', route)  7.88 us
    unnamed x12, local copies, waits for them, and re-layouts  2.86 us
    all_gather x1, blocking collectives, body(): lax.all_gather(one_back, 'pln')  2.18 us
    ppermute x2, starting transfers between devices, sibling(): return lax.ppermute(tile, 'pln', [(0, 1), (1, 0)])  0.65 us
  transfers between devices with their start and end apart: 4, of which 0 were waited for; matrix products, arithmetic and copies ran while one was open for 0% of the time, Pallas kernels for 28%

profile of v2, /device:TPU:0, one launch (start us, length us, event | category | flops | bytes accessed | tf_op | source)
XLA Modules:
  0.0 23.5 jit_solution(17306275177257045936)
XLA Ops:
  0.0 0.5 %collective-permute-start.2 = (f32[128,512]{1,0:T(8,128)}, f32[128,512]{1,0:T(8,128)S(1)}, u32[]{:S(2)}, u32[]{:S(2)}) collective-permute-start(f32[128,512]{1,0:T(8,128)} %bitcast.4), channel_id=1, source_target_pairs={{0,1},{1,0},{2,3},{3,2},{4,5},{5,4},{6,7},{7,6},{8,9},{9,8},{10,11... | collective-permute-start | bytes 786440 | tf_op jit(solution)/shard_map/ppermute | solution.py:201
  0.5 4.4 %collective-permute-start.1 = (f32[128,512]{1,0:T(8,128)}, f32[128,512]{1,0:T(8,128)S(1)}, u32[]{:S(2)}, u32[]{:S(2)}) collective-permute-start(f32[128,512]{1,0:T(8,128)} %bitcast.5), channel_id=1, source_target_pairs={{0,2},{2,4},{4,6},{6,8},{8,10},{10,12},{12,14},{1,3},{3,5},{5,7},{... | collective-permute-start | bytes 786440 | tf_op jit(solution)/shard_map/ppermute | solution.py:197
  4.9 3.5 %collective-permute-start = (f32[128,512]{1,0:T(8,128)}, f32[128,512]{1,0:T(8,128)S(1)}, u32[]{:S(2)}, u32[]{:S(2)}) collective-permute-start(f32[128,512]{1,0:T(8,128)} %bitcast.6), channel_id=1, source_target_pairs={{0,4},{2,6},{4,8},{6,10},{8,12},{10,14},{1,5},{3,7},{5,9},{7,11},{... | collective-permute-start | bytes 786440 | tf_op jit(solution)/shard_map/ppermute | solution.py:197
  8.3 0.0 collective-permute-done.2.other
  8.4 0.0 copy-start
  8.4 1.0 %copy-done = bf16[768,256]{1,0:T(8,128)(2,1)S(1)} copy-done((bf16[768,256]{1,0:T(8,128)(2,1)S(1)}, bf16[768,256]{1,0:T(8,128)(2,1)}, u32[]{:S(2)}) %copy-start) | copy-done | bytes 393240
  9.4 0.0 copy-start.1
  9.4 0.9 %copy-done.1 = bf16[272,256]{1,0:T(8,128)(2,1)S(1)} copy-done((bf16[272,256]{1,0:T(8,128)(2,1)S(1)}, bf16[272,256]{1,0:T(8,128)(2,1)}, u32[]{:S(2)}) %copy-start.1) | copy-done | bytes 139288
  10.3 0.0 copy-start.5
  10.3 0.9 %copy-done.5 = f32[1,128,512]{2,1,0:T(8,128)S(1)} copy-done((f32[1,128,512]{2,1,0:T(8,128)S(1)}, f32[1,128,512]{2,1,0:T(8,128)}, u32[]{:S(2)}) %copy-start.5) | copy-done | bytes 262168
  11.2 0.0 copy-start.2
  11.2 0.0 copy-start.3
  11.2 0.0 copy-start.4
  11.2 1.4 %shard_map.55.own = f32[3,528,256]{2,1,0:T(8,128)S(1)} custom-call(f32[128,512]{1,0:T(8,128)S(1)} %bitcast.7, f32[128,512]{1,0:T(8,128)S(1)} %collective-permute-done.2.other, bf16[272,256]{1,0:T(8,128)(2,1)S(1)} %copy-done.1, bf16[768,256]{1,0:T(8,128)(2,1)S(1)} %copy-done), custom_call_target="tpu_custom_call" | custom-call | flops 14000000 | bytes 42000 | tf_op jit(solution)/shard_map/pallas_call | solution.py:219
  12.6 0.0 collective-permute-done.1.mine
  12.6 2.2 %all-gather = f32[256,512]{1,0:T(8,128)S(1)} all-gather(f32[128,512]{1,0:T(8,128)S(1)} %collective-permute-done.1.mine), channel_id=2, replica_groups=mesh['blocks'=2,'sec'=8,'pln'=2] {'pln'}, dimensions={0}, use_global_device_ids=true | all-gather | bytes 786432 | tf_op jit(solution)/shard_map/all_gather | solution.py:231
  14.8 0.0 copy-done.2
  14.8 0.0 copy-done.3
  14.8 0.0 copy-done.4
  14.8 3.6 %shard_map.56.first = f32[3,32,8,128]{3,2,1,0:T(8,128)S(1)} custom-call(f32[128,512]{1,0:T(8,128)S(1)} %collective-permute-done.1.mine, f32[2,128,512]{2,1,0:T(8,128)S(1)} %bitcast.3, f32[3,528,256]{2,1,0:T(8,128)S(1)} %shard_map.55.own, bf16[272,256]{1,0:T(8,128)(2,1)S(1)} %copy-done.2, bf16[768,256]{1,0:T(8,128)(2,1)S(1)} %copy-done, ...), custom_call_target="tpu_custom_call" | custom-call | flops 36000000 | bytes 108000 | tf_op jit(solution)/shard_map/pallas_call | solution.py:219
  18.5 0.0 collective-permute-done.mine
  18.5 0.2 collective-permute-start.3
  18.7 1.4 %shard_map.57.outer = f32[32,8,128]{2,1,0:T(8,128)S(1)} custom-call(f32[128,512]{1,0:T(8,128)S(1)} %collective-permute-done.mine, f32[3,528,256]{2,1,0:T(8,128)S(1)} %shard_map.55.own, f32[3,32,8,128]{3,2,1,0:T(8,128)S(1)} %shard_map.56.first, bf16[272,256]{1,0:T(8,128)(2,1)S(1)} %copy-done.2, bf16[768,256]{1,0:T(8,128)(2,1)S(1)} %copy-done, ...), custom_call_target="tpu_custom_call" | custom-call | flops 15000000 | bytes 45000 | tf_op jit(solution)/shard_map/pallas_call | solution.py:219
  20.1 0.0 collective-permute-done.3.other
  20.1 3.4 %shard_map.58 = f32[2,8,4096]{2,1,0:T(8,128)} custom-call(f32[128,512]{1,0:T(8,128)S(1)} %collective-permute-done.mine, f32[128,512]{1,0:T(8,128)S(1)} %collective-permute-done.3.other, f32[3,528,256]{2,1,0:T(8,128)S(1)} %shard_map.55.own, f32[3,32,8,128]{3,2,1,0:T(8,128)S(1)} %shard_map.56.first, f32[32,8,128]{2,1,0:T(8,128)S(1)} %shard_map.57.outer, ...), custom_call_target="tpu_custom_call" | custom-call | flops 30000000 | bytes 90000 | tf_op jit(solution)/shard_map/pallas_call | solution.py:219
Async XLA Ops:
  0.0 8.4 %collective-permute-start.2 = (f32[128,512]{1,0:T(8,128)}, f32[128,512]{1,0:T(8,128)S(1)}, u32[]{:S(2)}, u32[]{:S(2)}) collective-permute-start(f32[128,512]{1,0:T(8,128)} %bitcast.4), channel_id=1, source_target_pairs={{0,1},{1,0},{2,3},{3,2},{4,5},{5,4},{6,7},{7,6},{8,9},{9,8},{10,11... | collective-permute-start | bytes 786440 | tf_op jit(solution)/shard_map/ppermute | solution.py:201
  0.5 12.2 %collective-permute-start.1 = (f32[128,512]{1,0:T(8,128)}, f32[128,512]{1,0:T(8,128)S(1)}, u32[]{:S(2)}, u32[]{:S(2)}) collective-permute-start(f32[128,512]{1,0:T(8,128)} %bitcast.5), channel_id=1, source_target_pairs={{0,2},{2,4},{4,6},{6,8},{8,10},{10,12},{12,14},{1,3},{3,5},{5,7},{... | collective-permute-start | bytes 786440 | tf_op jit(solution)/shard_map/ppermute | solution.py:197
  4.9 13.6 %collective-permute-start = (f32[128,512]{1,0:T(8,128)}, f32[128,512]{1,0:T(8,128)S(1)}, u32[]{:S(2)}, u32[]{:S(2)}) collective-permute-start(f32[128,512]{1,0:T(8,128)} %bitcast.6), channel_id=1, source_target_pairs={{0,4},{2,6},{4,8},{6,10},{8,12},{10,14},{1,5},{3,7},{5,9},{7,11},{... | collective-permute-start | bytes 786440 | tf_op jit(solution)/shard_map/ppermute | solution.py:197
  8.4 1.0 %copy-start = (bf16[768,256]{1,0:T(8,128)(2,1)S(1)}, bf16[768,256]{1,0:T(8,128)(2,1)}, u32[]{:S(2)}) copy-start(bf16[768,256]{1,0:T(8,128)(2,1)} %constant.9.clone.cols) | copy-start | bytes 1179652
  9.4 0.9 %copy-start.1 = (bf16[272,256]{1,0:T(8,128)(2,1)S(1)}, bf16[272,256]{1,0:T(8,128)(2,1)}, u32[]{:S(2)}) copy-start(bf16[272,256]{1,0:T(8,128)(2,1)} %constant.8.clone.rows) | copy-start | bytes 417796
  10.3 0.9 %copy-start.5 = (f32[1,128,512]{2,1,0:T(8,128)S(1)}, f32[1,128,512]{2,1,0:T(8,128)}, u32[]{:S(2)}) copy-start(f32[1,128,512]{2,1,0:T(8,128)} %param.5) | copy-start | bytes 786436
  11.2 3.6 %copy-start.2 = (bf16[272,256]{1,0:T(8,128)(2,1)S(1)}, bf16[272,256]{1,0:T(8,128)(2,1)}, u32[]{:S(2)}) copy-start(bf16[272,256]{1,0:T(8,128)(2,1)} %constant.8.clone.rows) | copy-start | bytes 417796
  11.2 3.6 %copy-start.3 = (bf16[256,256]{1,0:T(8,128)(2,1)S(1)}, bf16[256,256]{1,0:T(8,128)(2,1)}, u32[]{:S(2)}) copy-start(bf16[256,256]{1,0:T(8,128)(2,1)} %constant.11.clone.back_cols) | copy-start | bytes 393220
  11.2 3.6 %copy-start.4 = (bf16[128,192]{1,0:T(8,128)(2,1)S(1)}, bf16[128,192]{1,0:T(8,128)(2,1)}, u32[]{:S(2)}) copy-start(bf16[128,192]{1,0:T(8,128)(2,1)} %constant.10.clone.back_rows) | copy-start | bytes 147460
  18.5 1.6 %collective-permute-start.3 = (f32[128,512]{1,0:T(8,128)S(1)}, f32[128,512]{1,0:T(8,128)S(1)}, u32[]{:S(2)}, u32[]{:S(2)}) collective-permute-start(f32[128,512]{1,0:T(8,128)S(1)} %collective-permute-done.mine), channel_id=1, source_target_pairs={{0,1},{1,0},{2,3},{3,2},{4,5},{5,4},{6,7},{7,6},{8,9},{9,8},{10,11... | collective-permute-start | bytes 786440 | tf_op jit(solution)/shard_map/ppermute | solution.py:201

commit v3 on v2

--- a/solution.py
+++ b/solution.py
@@ -51,8 +51,10 @@
     weight = np.where(freq == 0, 1.0, 2.0) / PATCH**3
     angle = turn * (np.outer(ordered, freq) % PATCH)
     high, low = high_low(np.concatenate([np.cos(angle) * weight, -np.sin(angle) * weight]))
-    back_rows = np.concatenate([high, high, low], 1)
-    return rows, cols, back_rows, back_cols
+    back_rows = np.concatenate([high, high, low, low], 1)
+    parts = (rows, cols, back_rows, back_cols)
+    ends = np.cumsum([len(x) for x in parts])
+    return np.concatenate(parts), [slice(int(end) - len(x), int(end)) for x, end in zip(parts, ends)]
 
 
 def dot(left, right):
@@ -76,10 +78,10 @@
     return [jnp.concatenate([first, x[MARGIN:-MARGIN], last]) for x in (mine, other)]
 
 
-def spectrum(pixels, rows, cols, left):
+def expand(pixels, rows, left):
     tiles = pixels.shape[1] // LANES
     patches = pixels.shape[1] // STRIDE
-    found = dot(rows, jnp.concatenate(split(pixels)))
+    found = dot(rows[...], jnp.concatenate(split(pixels)))
     parts = split(found[:PATCH] + found[PATCH + NYQ :])
     middle = found[PATCH : PATCH + 8]
     lane = lax.broadcasted_iota(jnp.int32, (PATCH, LANES), 1)
@@ -115,24 +117,34 @@
     for base, value in zip((0, width, 2 * width), (high, low, high)):
         left[at, base : base + PATCH] = value
         left[at, base + PATCH : base + width] = blank
-    return dot(left[...], cols[...])
-
-
-def surface(own, back, back_rows, back_cols, right, lagged):
-    patches = (own.shape[0] - NYQ) // HALF
+
+
+def spectra(pixels, rows, cols, left, out):
+    for r, x in enumerate(pixels):
+        expand(x, rows, left.at[r])
+    for r in range(len(pixels)):
+        out[r] = dot(left[r], cols[...])
+
+
+def multiply(own, back, back_cols, half):
+    size = own.shape[0]
     xr, xi = own[:, :PATCH], own[:, PATCH:]
     yr, yi = back[:, :PATCH], back[:, PATCH:]
     product = jnp.concatenate([xr * yr + xi * yi, xi * yr - xr * yi], 1)
     found = dot(jnp.concatenate(split(product)), back_cols[...])
-    size = own.shape[0]
-    found = (found[:size, :LANES] + found[size:, :LANES]) + (found[:size, LANES:] + found[size:, LANES:])
-    high, low = split(found[: patches * HALF])
+    half[...] = (found[:size, :LANES] + found[size:, :LANES]) + (found[:size, LANES:] + found[size:, LANES:])
+
+
+def finish(half, back_rows, right, lagged):
+    patches = (half.shape[0] - NYQ) // HALF
+    high, low = split(half[: patches * HALF])
     for j in range(patches):
         at, lanes = slice(j * HALF, (j + 1) * HALF), slice(j * LANES, (j + 1) * LANES)
         right[:HALF, lanes] = high[at]
         right[HALF : 2 * HALF, lanes] = low[at]
-        right[2 * HALF :, lanes] = high[at]
-    middle = found[patches * HALF : patches * HALF + patches] * (1.0 / PATCH**3)
+        right[2 * HALF : 3 * HALF, lanes] = high[at]
+        right[3 * HALF :, lanes] = low[at]
+    middle = half[patches * HALF : patches * HALF + patches] * (1.0 / PATCH**3)
     found = dot(back_rows[...], right[...])
     lane = lax.broadcasted_iota(jnp.int32, (PAIRS, LANES), 1)
     for j in range(patches):
@@ -145,19 +157,40 @@
     return lagged[...].reshape(PAIRS, patches, LANES) + middle[None]
 
 
-def own_kernel(mine, other, rows, cols, out, left):
+def surfaces(pixels, own, rows, cols, back_rows, back_cols, left, spec, half, right, lagged):
+    spectra(pixels, rows, cols, left, spec)
+    for r in range(len(pixels)):
+        multiply(own(r), spec[r], back_cols, half.at[r])
+    return lambda r: finish(half.at[r], back_rows, right.at[r], lagged.at[r])
+
+
+def own_kernel(at, mine, other, table, out, left, *_):
+    rows, cols = table.at[at[0]], table.at[at[1]]
     lower = lax.axis_index("pln") == 1
     mine, other = mine[...], other[...]
-    for r, pixels in enumerate([outer_row(mine, lower)] + inner_rows(mine, other, lower)):
-        out[r] = spectrum(pixels, rows[...], cols, left.at[r])
-
-
-def first_kernel(mine, other, own, rows, cols, back_rows, back_cols, out, left, right, lagged):
-    lower = lax.axis_index("pln") == 1
-    mine, other = mine[...], other[1 - lax.axis_index("pln")]
-    for r, pixels in enumerate([outer_row(mine, lower)] + inner_rows(mine, other, lower)):
-        back = spectrum(pixels, rows[...], cols, left.at[r])
-        out[r] = surface(own[r], back, back_rows, back_cols, right.at[r], lagged.at[r])
+    spectra([outer_row(mine, lower)] + inner_rows(mine, other, lower), rows, cols, left, out)
+
+
+def reached(distance, work):
+    present = lax.axis_index("sec") >= distance
+    pl.when(present)(lambda: work(True))
+    pl.when(jnp.logical_not(present))(lambda: work(False))
+
+
+def first_kernel(at, mine, both, own, table, out, *scratch):
+    pln = lax.axis_index("pln")
+
+    def work(present):
+        if not present:
+            out[...] = jnp.zeros_like(out)
+            return
+        here, there = mine[...], both[1 - pln]
+        pixels = [outer_row(here, pln == 1)] + inner_rows(here, there, pln == 1)
+        found = surfaces(pixels, lambda r: own[r], *(table.at[x] for x in at), *scratch)
+        for r in range(len(pixels)):
+            out[r] = found(r)
+
+    reached(1, work)
 
 
 def joined_row(one, two):
@@ -169,26 +202,37 @@
     return (2.0 * joined + before + after) * (1.0 / 16.0)
 
 
-def outer_kernel(mine, own, first, rows, cols, back_rows, back_cols, out, left, right, lagged):
-    lower = lax.axis_index("pln") == 1
-    back = spectrum(outer_row(mine[...], lower), rows[...], cols, left)
-    out[...] = joined_row(first[0], surface(own[0], back, back_rows, back_cols, right, lagged))
-
-
-def inner_kernel(mine, other, own, first, outer, rows, cols, back_rows, back_cols, out, left, right, lagged):
+def outer_kernel(at, mine, own, first, table, out, *scratch):
+    def work(present):
+        found = jnp.zeros_like
+        if present:
+            pixels = [outer_row(mine[...], lax.axis_index("pln") == 1)]
+            got = surfaces(pixels, lambda r: own[r], *(table.at[x] for x in at), *scratch)
+            found = lambda _: got(0)
+        one = first[0]
+        out[...] = joined_row(one, found(one))
+
+    reached(2, work)
+
+
+def inner_kernel(at, mine, other, own, first, outer, table, out, *scratch):
     pln = lax.axis_index("pln")
-    mixed = []
-    for r, pixels in enumerate(inner_rows(mine[...], other[...], pln == 1)):
-        back = spectrum(pixels, rows[...], cols, left.at[r])
-        two = surface(own[r + 1], back, back_rows, back_cols, right.at[r], lagged.at[r])
-        mixed.append(joined_row(first[r + 1], two))
-    ending = outer[...]
-    ends = 2.0 * ending + mixed[0]
-    inside = ending + 2.0 * mixed[0] + mixed[1]
-    for pair in range(PAIRS):
-        lanes = slice(pair * LANES, (pair + 1) * LANES)
-        out[pln, :, lanes] = ends[pair]
-        out[1 - pln, :, lanes] = inside[pair]
+
+    def work(present):
+        found = lambda r: jnp.zeros(outer.shape, F32)
+        if present:
+            pixels = inner_rows(mine[...], other[...], pln == 1)
+            found = surfaces(pixels, lambda r: own[r + 1], *(table.at[x] for x in at), *scratch)
+        near, far = (joined_row(first[r + 1], found(r)) for r in range(2))
+        ending = outer[...]
+        ends = 2.0 * ending + near
+        inside = ending + 2.0 * near + far
+        for pair in range(PAIRS):
+            lanes = slice(pair * LANES, (pair + 1) * LANES)
+            out[pln, :, lanes] = ends[pair]
+            out[1 - pln, :, lanes] = inside[pair]
+
+    reached(2, work)
 
 
 def from_sections(tile, distance, ring):
@@ -206,35 +250,34 @@
     height, width = tile.shape
     patches = width // STRIDE
     assert height == PATCH and lax.axis_size("pln") == 2 and patches == 8
-    rows, cols, back_rows, back_cols = tables()
+    table, at = tables()
     packed = patches * HALF + NYQ
-    surfaces = (PAIRS, patches, LANES)
-
-    def call(kernel, shape, spread, micros, *args):
+    shape = (PAIRS, patches, LANES)
+
+    def call(kernel, shape, spread, *args):
         scratch = [
-            pltpu.VMEM(spread + (packed, 6 * PATCH), BF16),
-            pltpu.VMEM(spread + (3 * HALF, patches * LANES), BF16),
-            pltpu.VMEM(spread + (PAIRS * patches, LANES), F32),
+            pltpu.VMEM((spread, packed, 6 * PATCH), BF16),
+            pltpu.VMEM((spread, packed, 2 * PATCH), F32),
+            pltpu.VMEM((spread, packed, LANES), F32),
+            pltpu.VMEM((spread, 4 * HALF, patches * LANES), BF16),
+            pltpu.VMEM((spread, PAIRS * patches, LANES), F32),
         ]
         return pl.pallas_call(
-            kernel,
+            functools.partial(kernel, at),
             out_shape=jax.ShapeDtypeStruct(shape, F32),
-            scratch_shapes=scratch[:1] if kernel is own_kernel else scratch,
-            cost_estimate=pl.CostEstimate(flops=int(micros * 1e7), bytes_accessed=int(micros * 3e4), transcendentals=0),
-            compiler_params=pltpu.CompilerParams(vmem_limit_bytes=48 * 2**20),
+            scratch_shapes=scratch,
+            compiler_params=pltpu.CompilerParams(vmem_limit_bytes=40 * 2**20),
         )(*args)
 
-    one_back = from_sections(tile, 1, False)
-    two_back = from_sections(tile, 2, False)
-    own = call(own_kernel, (3, packed, 2 * PATCH), (3,), 1.4, tile, sibling(tile), rows, cols)
+    one_back = from_sections(tile, 1, True)
+    own = call(own_kernel, (3, packed, 2 * PATCH), 3, tile, sibling(tile), table)
+    two_back = from_sections(tile, 2, True)
     one_back, own = lax.optimization_barrier((one_back, own))
-    first = call(first_kernel, (3,) + surfaces, (3,), 3.6, one_back, lax.all_gather(one_back, 'pln'), own, rows, cols, back_rows, back_cols)
+    first = call(first_kernel, (3,) + shape, 3, one_back, lax.all_gather(one_back, "pln"), own, table)
     two_back, first = lax.optimization_barrier((two_back, first))
     other = sibling(two_back)
-    outer = call(outer_kernel, surfaces, (), 1.5, two_back, own, first, rows, cols, back_rows, back_cols)
-    mixed = call(
-        inner_kernel, (2, patches, CROP * CROP), (2,), 3.0, two_back, other, own, first, outer, rows, cols, back_rows, back_cols
-    )
+    outer = call(outer_kernel, shape, 1, two_back, own, first, table)
+    mixed = call(inner_kernel, (2, patches, CROP * CROP), 2, two_back, other, own, first, outer, table)
     return mixed[None]
 
 

time: 23.7 us -> 19.4 us (0.82)
  the two profiles are of different devices: /device:TPU:0 before, /device:TPU:11 now
where the time goes in v3:
time: 19.4 us; the launch traced here: 19.1 us
  Pallas kernels  7.19 us (37%)
  starting transfers between devices  4.02 us (21%)
  waiting for transfers between devices  3.22 us (17%)
  blocking collectives  2.58 us (13%)
  local copies, waits for them, and re-layouts  2.06 us (11%)
    pallas_call x4, Pallas kernels, call(): pl.pallas_call(functools.partial(kernel, at), out_shape=jax.ShapeDtypeStr...  7.19 us
    ppermute x2, waiting for transfers between devices, from_sections(): return lax.ppermute(tile, 'sec', route)  3.21 us
    all_gather x1, blocking collectives, body(): lax.all_gather(one_back, 'pln')  2.58 us
    ppermute x2, starting transfers between devices, from_sections(): return lax.ppermute(tile, 'sec', route)  2.56 us
    unnamed x4, local copies, waits for them, and re-layouts  2.06 us
    ppermute x2, starting transfers between devices, sibling(): return lax.ppermute(tile, 'pln', [(0, 1), (1, 0)])  1.46 us
  transfers between devices with their start and end apart: 4, of which 2 were waited for; matrix products, arithmetic and copies ran while one was open for 0% of the time, Pallas kernels for 25%

profile of v3, /device:TPU:11, one launch (start us, length us, event | category | flops | bytes accessed | tf_op | source)
XLA Modules:
  0.0 19.1 jit_solution(886107545861014796)
XLA Ops:
  0.0 0.7 %collective-permute-start.2 = (f32[128,512]{1,0:T(8,128)}, f32[128,512]{1,0:T(8,128)S(1)}, u32[]{:S(2)}, u32[]{:S(2)}) collective-permute-start(f32[128,512]{1,0:T(8,128)} %bitcast.4), channel_id=1, source_target_pairs={{0,1},{1,0},{2,3},{3,2},{4,5},{5,4},{6,7},{7,6},{8,9},{9,8},{10,11... | collective-permute-start | bytes 786440 | tf_op jit(solution)/shard_map/ppermute | solution.py:245
  0.7 1.3 %collective-permute-start.1 = (f32[128,512]{1,0:T(8,128)}, f32[128,512]{1,0:T(8,128)S(1)}, u32[]{:S(2)}, u32[]{:S(2)}) collective-permute-start(f32[128,512]{1,0:T(8,128)} %bitcast.5), channel_id=1, source_target_pairs={{0,2},{2,4},{4,6},{6,8},{8,10},{10,12},{12,14},{14,0},{1,3},{3,5},... | collective-permute-start | bytes 786440 | tf_op jit(solution)/shard_map/ppermute | solution.py:241
  1.9 1.3 %collective-permute-start = (f32[128,512]{1,0:T(8,128)}, f32[128,512]{1,0:T(8,128)S(1)}, u32[]{:S(2)}, u32[]{:S(2)}) collective-permute-start(f32[128,512]{1,0:T(8,128)} %bitcast.6), channel_id=1, source_target_pairs={{0,4},{2,6},{4,8},{6,10},{8,12},{10,14},{12,0},{14,2},{1,5},{3,7},... | collective-permute-start | bytes 786440 | tf_op jit(solution)/shard_map/ppermute | solution.py:241
  3.2 0.0 collective-permute-done.2.other
  3.2 0.0 copy-start
  3.2 1.1 %copy-done = bf16[1424,256]{1,0:T(8,128)(2,1)S(1)} copy-done((bf16[1424,256]{1,0:T(8,128)(2,1)S(1)}, bf16[1424,256]{1,0:T(8,128)(2,1)}, u32[]{:S(2)}) %copy-start) | copy-done | bytes 729112
  4.4 0.0 copy-start.1
  4.4 0.9 %copy-done.1 = f32[1,128,512]{2,1,0:T(8,128)S(1)} copy-done((f32[1,128,512]{2,1,0:T(8,128)S(1)}, f32[1,128,512]{2,1,0:T(8,128)}, u32[]{:S(2)}) %copy-start.1) | copy-done | bytes 262168
  5.3 1.2 %shard_map.28.own = f32[3,528,256]{2,1,0:T(8,128)S(1)} custom-call(f32[128,512]{1,0:T(8,128)S(1)} %bitcast.7, f32[128,512]{1,0:T(8,128)S(1)} %collective-permute-done.2.other, bf16[1424,256]{1,0:T(8,128)(2,1)S(1)} %copy-done), custom_call_target="tpu_custom_call" | custom-call | tf_op jit(solution)/shard_map/pallas_call | solution.py:265
  6.5 2.3 %collective-permute-done.1.mine = f32[128,512]{1,0:T(8,128)S(1)} collective-permute-done((f32[128,512]{1,0:T(8,128)}, f32[128,512]{1,0:T(8,128)S(1)}, u32[]{:S(2)}, u32[]{:S(2)}) %collective-permute-start.1) | collective-permute-done | bytes 262176 | tf_op jit(solution)/shard_map/ppermute | solution.py:241
  8.8 2.6 %all-gather = f32[256,512]{1,0:T(8,128)S(1)} all-gather(f32[128,512]{1,0:T(8,128)S(1)} %collective-permute-done.1.mine), channel_id=2, replica_groups=mesh['blocks'=2,'sec'=8,'pln'=2] {'pln'}, dimensions={0}, use_global_device_ids=true | all-gather | bytes 786432 | tf_op jit(solution)/shard_map/all_gather | solution.py:276
  11.4 2.1 %shard_map.29.first = f32[3,32,8,128]{3,2,1,0:T(8,128)S(1)} custom-call(f32[128,512]{1,0:T(8,128)S(1)} %collective-permute-done.1.mine, f32[2,128,512]{2,1,0:T(8,128)S(1)} %bitcast.3, f32[3,528,256]{2,1,0:T(8,128)S(1)} %shard_map.28.own, bf16[1424,256]{1,0:T(8,128)(2,1)S(1)} %copy-done), custom_call_target="tpu_custom_call" | custom-call | tf_op jit(solution)/shard_map/pallas_call | solution.py:265
  13.5 0.9 %collective-permute-done.mine = f32[128,512]{1,0:T(8,128)S(1)} collective-permute-done((f32[128,512]{1,0:T(8,128)}, f32[128,512]{1,0:T(8,128)S(1)}, u32[]{:S(2)}, u32[]{:S(2)}) %collective-permute-start) | collective-permute-done | bytes 262176 | tf_op jit(solution)/shard_map/ppermute | solution.py:241
  14.4 0.8 %collective-permute-start.3 = (f32[128,512]{1,0:T(8,128)S(1)}, f32[128,512]{1,0:T(8,128)S(1)}, u32[]{:S(2)}, u32[]{:S(2)}) collective-permute-start(f32[128,512]{1,0:T(8,128)S(1)} %collective-permute-done.mine), channel_id=1, source_target_pairs={{0,1},{1,0},{2,3},{3,2},{4,5},{5,4},{6,7},{7,6},{8,9},{9,8},{10,11... | collective-permute-start | bytes 786440 | tf_op jit(solution)/shard_map/ppermute | solution.py:245
  15.2 1.5 %shard_map.30.outer = f32[32,8,128]{2,1,0:T(8,128)S(1)} custom-call(f32[128,512]{1,0:T(8,128)S(1)} %collective-permute-done.mine, f32[3,528,256]{2,1,0:T(8,128)S(1)} %shard_map.28.own, f32[3,32,8,128]{3,2,1,0:T(8,128)S(1)} %shard_map.29.first, bf16[1424,256]{1,0:T(8,128)(2,1)S(1)} %copy-done), custom_call_target="tpu_custom_call" | custom-call | tf_op jit(solution)/shard_map/pallas_call | solution.py:265
  16.7 0.0 collective-permute-done.3.other
  16.7 2.4 %shard_map.31 = f32[2,8,4096]{2,1,0:T(8,128)} custom-call(f32[128,512]{1,0:T(8,128)S(1)} %collective-permute-done.mine, f32[128,512]{1,0:T(8,128)S(1)} %collective-permute-done.3.other, f32[3,528,256]{2,1,0:T(8,128)S(1)} %shard_map.28.own, f32[3,32,8,128]{3,2,1,0:T(8,128)S(1)} %shard_map.29.first, f32[32,8,128]{2,1,0:T(8,128)S(1)} %shard_map.30.outer, ...), custom_call_target="tpu_custom_call" | custom-call | tf_op jit(solution)/shard_map/pallas_call | solution.py:265
Async XLA Ops:
  0.0 3.2 %collective-permute-start.2 = (f32[128,512]{1,0:T(8,128)}, f32[128,512]{1,0:T(8,128)S(1)}, u32[]{:S(2)}, u32[]{:S(2)}) collective-permute-start(f32[128,512]{1,0:T(8,128)} %bitcast.4), channel_id=1, source_target_pairs={{0,1},{1,0},{2,3},{3,2},{4,5},{5,4},{6,7},{7,6},{8,9},{9,8},{10,11... | collective-permute-start | bytes 786440 | tf_op jit(solution)/shard_map/ppermute | solution.py:245
  0.7 8.1 %collective-permute-start.1 = (f32[128,512]{1,0:T(8,128)}, f32[128,512]{1,0:T(8,128)S(1)}, u32[]{:S(2)}, u32[]{:S(2)}) collective-permute-start(f32[128,512]{1,0:T(8,128)} %bitcast.5), channel_id=1, source_target_pairs={{0,2},{2,4},{4,6},{6,8},{8,10},{10,12},{12,14},{14,0},{1,3},{3,5},... | collective-permute-start | bytes 786440 | tf_op jit(solution)/shard_map/ppermute | solution.py:241
  1.9 12.5 %collective-permute-start = (f32[128,512]{1,0:T(8,128)}, f32[128,512]{1,0:T(8,128)S(1)}, u32[]{:S(2)}, u32[]{:S(2)}) collective-permute-start(f32[128,512]{1,0:T(8,128)} %bitcast.6), channel_id=1, source_target_pairs={{0,4},{2,6},{4,8},{6,10},{8,12},{10,14},{12,0},{14,2},{1,5},{3,7},... | collective-permute-start | bytes 786440 | tf_op jit(solution)/shard_map/ppermute | solution.py:241
  3.2 1.1 %copy-start = (bf16[1424,256]{1,0:T(8,128)(2,1)S(1)}, bf16[1424,256]{1,0:T(8,128)(2,1)}, u32[]{:S(2)}) copy-start(bf16[1424,256]{1,0:T(8,128)(2,1)} %constant.2.clone.table) | copy-start | bytes 2187268
  4.4 0.9 %copy-start.1 = (f32[1,128,512]{2,1,0:T(8,128)S(1)}, f32[1,128,512]{2,1,0:T(8,128)}, u32[]{:S(2)}) copy-start(f32[1,128,512]{2,1,0:T(8,128)} %param.2) | copy-start | bytes 786436
  14.4 2.2 %collective-permute-start.3 = (f32[128,512]{1,0:T(8,128)S(1)}, f32[128,512]{1,0:T(8,128)S(1)}, u32[]{:S(2)}, u32[]{:S(2)}) collective-permute-start(f32[128,512]{1,0:T(8,128)S(1)} %collective-permute-done.mine), channel_id=1, source_target_pairs={{0,1},{1,0},{2,3},{3,2},{4,5},{5,4},{6,7},{7,6},{8,9},{9,8},{10,11... | collective-permute-start | bytes 786440 | tf_op jit(solution)/shard_map/ppermute | solution.py:245

commit v4 on v3

--- a/solution.py
+++ b/solution.py
@@ -135,15 +135,17 @@
     half[...] = (found[:size, :LANES] + found[size:, :LANES]) + (found[:size, LANES:] + found[size:, LANES:])
 
 
-def finish(half, back_rows, right, lagged):
+def stack(half, right):
     patches = (half.shape[0] - NYQ) // HALF
     high, low = split(half[: patches * HALF])
     for j in range(patches):
         at, lanes = slice(j * HALF, (j + 1) * HALF), slice(j * LANES, (j + 1) * LANES)
-        right[:HALF, lanes] = high[at]
-        right[HALF : 2 * HALF, lanes] = low[at]
-        right[2 * HALF : 3 * HALF, lanes] = high[at]
-        right[3 * HALF :, lanes] = low[at]
+        for q, value in enumerate((high, low, high, low)):
+            right[q * HALF : (q + 1) * HALF, lanes] = value[at]
+
+
+def finish(half, back_rows, right, lagged):
+    patches = (half.shape[0] - NYQ) // HALF
     middle = half[patches * HALF : patches * HALF + patches] * (1.0 / PATCH**3)
     found = dot(back_rows[...], right[...])
     lane = lax.broadcasted_iota(jnp.int32, (PAIRS, LANES), 1)
@@ -161,13 +163,15 @@
     spectra(pixels, rows, cols, left, spec)
     for r in range(len(pixels)):
         multiply(own(r), spec[r], back_cols, half.at[r])
+    for r in range(len(pixels)):
+        stack(half.at[r], right.at[r])
     return lambda r: finish(half.at[r], back_rows, right.at[r], lagged.at[r])
 
 
 def own_kernel(at, mine, other, table, out, left, *_):
     rows, cols = table.at[at[0]], table.at[at[1]]
     lower = lax.axis_index("pln") == 1
-    mine, other = mine[...], other[...]
+    mine, other = mine[...], other[1 - lax.axis_index("pln")]
     spectra([outer_row(mine, lower)] + inner_rows(mine, other, lower), rows, cols, left, out)
 
 
@@ -185,7 +189,7 @@
             out[...] = jnp.zeros_like(out)
             return
         here, there = mine[...], both[1 - pln]
-        pixels = [outer_row(here, pln == 1)] + inner_rows(here, there, pln == 1)
+        pixels = [outer_row(here, pln == 1)] + inner_rows(here, there, pln == 1)[:1]
         found = surfaces(pixels, lambda r: own[r], *(table.at[x] for x in at), *scratch)
         for r in range(len(pixels)):
             out[r] = found(r)
@@ -202,35 +206,48 @@
     return (2.0 * joined + before + after) * (1.0 / 16.0)
 
 
-def outer_kernel(at, mine, own, first, table, out, *scratch):
+def outer_kernel(at, mine, earlier, both, own, first, table, out, far, *scratch):
+    pln, sec = lax.axis_index("pln"), lax.axis_index("sec")
+
     def work(present):
-        found = jnp.zeros_like
+        parts = [table.at[x] for x in at]
+        beyond = inner_rows(earlier[...], both[1 - pln], pln == 1)[1]
+        one = first[0]
         if present:
-            pixels = [outer_row(mine[...], lax.axis_index("pln") == 1)]
-            got = surfaces(pixels, lambda r: own[r], *(table.at[x] for x in at), *scratch)
-            found = lambda _: got(0)
-        one = first[0]
-        out[...] = joined_row(one, found(one))
+            got = surfaces([outer_row(mine[...], pln == 1), beyond], lambda r: own[2 * r], *parts, *scratch)
+            out[...] = joined_row(one, got(0))
+            far[...] = got(1)
+        else:
+            got = surfaces([beyond], lambda r: own[2], *parts, *scratch)
+            out[...] = joined_row(one, jnp.zeros_like(one))
+            far[...] = jnp.where(sec >= 1, got(0), 0.0)
 
     reached(2, work)
 
 
-def inner_kernel(at, mine, other, own, first, outer, table, out, *scratch):
+def inner_kernel(at, mine, other, own, first, outer, beyond, table, out, left, spec, half, right, lagged, staged, sent):
     pln = lax.axis_index("pln")
+
+    def send(slot, row, value):
+        for pair in range(PAIRS):
+            staged[slot, :, pair * LANES : (pair + 1) * LANES] = value[pair]
+        copy = pltpu.make_async_copy(staged.at[slot], out.at[row], sent.at[slot])
+        copy.start()
+        return copy
 
     def work(present):
         found = lambda r: jnp.zeros(outer.shape, F32)
         if present:
             pixels = inner_rows(mine[...], other[...], pln == 1)
-            found = surfaces(pixels, lambda r: own[r + 1], *(table.at[x] for x in at), *scratch)
-        near, far = (joined_row(first[r + 1], found(r)) for r in range(2))
+            parts = (table.at[x] for x in at)
+            found = surfaces(pixels, lambda r: own[r + 1], *parts, left, spec, half, right, lagged)
+        near = joined_row(first[1], found(0))
         ending = outer[...]
-        ends = 2.0 * ending + near
-        inside = ending + 2.0 * near + far
-        for pair in range(PAIRS):
-            lanes = slice(pair * LANES, (pair + 1) * LANES)
-            out[pln, :, lanes] = ends[pair]
-            out[1 - pln, :, lanes] = inside[pair]
+        copies = [send(0, pln, 2.0 * ending + near)]
+        far = joined_row(beyond[...], found(1))
+        copies.append(send(1, 1 - pln, ending + 2.0 * near + far))
+        for copy in copies:
+            copy.wait()
 
     reached(2, work)
 
@@ -254,7 +271,7 @@
     packed = patches * HALF + NYQ
     shape = (PAIRS, patches, LANES)
 
-    def call(kernel, shape, spread, *args):
+    def call(kernel, shape, spread, *args, outs=1):
         scratch = [
             pltpu.VMEM((spread, packed, 6 * PATCH), BF16),
             pltpu.VMEM((spread, packed, 2 * PATCH), F32),
@@ -262,22 +279,25 @@
             pltpu.VMEM((spread, 4 * HALF, patches * LANES), BF16),
             pltpu.VMEM((spread, PAIRS * patches, LANES), F32),
         ]
+        ending = [pltpu.VMEM(shape, F32), pltpu.SemaphoreType.DMA((2,))] if kernel is inner_kernel else []
         return pl.pallas_call(
             functools.partial(kernel, at),
-            out_shape=jax.ShapeDtypeStruct(shape, F32),
-            scratch_shapes=scratch,
+            out_shape=[jax.ShapeDtypeStruct(shape, F32)] * outs,
+            out_specs=[pl.BlockSpec(memory_space=pl.ANY if ending else pltpu.VMEM)] * outs,
+            scratch_shapes=scratch + ending,
             compiler_params=pltpu.CompilerParams(vmem_limit_bytes=40 * 2**20),
         )(*args)
 
     one_back = from_sections(tile, 1, True)
-    own = call(own_kernel, (3, packed, 2 * PATCH), 3, tile, sibling(tile), table)
     two_back = from_sections(tile, 2, True)
+    (own,) = call(own_kernel, (3, packed, 2 * PATCH), 3, tile, lax.all_gather(tile, "pln"), table)
     one_back, own = lax.optimization_barrier((one_back, own))
-    first = call(first_kernel, (3,) + shape, 3, one_back, lax.all_gather(one_back, "pln"), own, table)
+    both = lax.all_gather(one_back, "pln")
+    (first,) = call(first_kernel, (2,) + shape, 2, one_back, both, own, table)
     two_back, first = lax.optimization_barrier((two_back, first))
     other = sibling(two_back)
-    outer = call(outer_kernel, shape, 1, two_back, own, first, table)
-    mixed = call(inner_kernel, (2, patches, CROP * CROP), 2, two_back, other, own, first, outer, table)
+    outer, beyond = call(outer_kernel, shape, 2, two_back, one_back, both, own, first, table, outs=2)
+    (mixed,) = call(inner_kernel, (2, patches, CROP * CROP), 2, two_back, other, own, first, outer, beyond, table)
     return mixed[None]
 
 

time: 19.4 us -> 19.1 us (0.985)
  the two profiles are of different devices: /device:TPU:11 before, /device:TPU:13 now
where the time goes in v4:
time: 19.1 us; the launch traced here: 18.9 us
  blocking collectives  7 us (37%)
  Pallas kernels  6.83 us (36%)
  starting transfers between devices  2.95 us (15%)
  local copies, waits for them, and re-layouts  2.06 us (11%)
    pallas_call x4, Pallas kernels, call(): pl.pallas_call(functools.partial(kernel, at), out_shape=[jax.ShapeDtypeSt...  6.83 us
    all_gather x1, blocking collectives, body(): both = lax.all_gather(one_back, 'pln')  3.76 us
    all_gather x1, blocking collectives, body(): lax.all_gather(tile, 'pln')  3.24 us
    ppermute x2, starting transfers between devices, from_sections(): return lax.ppermute(tile, 'sec', route)  2.51 us
    unnamed x4, local copies, waits for them, and re-layouts  2.06 us
    ppermute x1, starting transfers between devices, sibling(): return lax.ppermute(tile, 'pln', [(0, 1), (1, 0)])  0.44 us
  transfers between devices with their start and end apart: 3, of which 0 were waited for; matrix products, arithmetic and copies ran while one was open for 0% of the time, Pallas kernels for 23%

profile of v4, /device:TPU:13, one launch (start us, length us, event | category | flops | bytes accessed | tf_op | source)
XLA Modules:
  0.0 18.9 jit_solution(5075492823921501736)
XLA Ops:
  0.0 1.2 %collective-permute-start.1 = (f32[128,512]{1,0:T(8,128)}, f32[128,512]{1,0:T(8,128)S(1)}, u32[]{:S(2)}, u32[]{:S(2)}) collective-permute-start(f32[128,512]{1,0:T(8,128)} %bitcast.5), channel_id=1, source_target_pairs={{0,2},{2,4},{4,6},{6,8},{8,10},{10,12},{12,14},{14,0},{1,3},{3,5},... | collective-permute-start | bytes 786440 | tf_op jit(solution)/shard_map/ppermute | solution.py:258
  1.2 1.3 %collective-permute-start = (f32[128,512]{1,0:T(8,128)}, f32[128,512]{1,0:T(8,128)S(1)}, u32[]{:S(2)}, u32[]{:S(2)}) collective-permute-start(f32[128,512]{1,0:T(8,128)} %bitcast.6), channel_id=1, source_target_pairs={{0,4},{2,6},{4,8},{6,10},{8,12},{10,14},{12,0},{14,2},{1,5},{3,7},... | collective-permute-start | bytes 786440 | tf_op jit(solution)/shard_map/ppermute | solution.py:258
  2.5 3.2 %all_gather.9.other = f32[2,128,512]{2,1,0:T(8,128)S(1)} all-gather(f32[1,128,512]{2,1,0:T(8,128)} %param.2), channel_id=1, replica_groups=mesh['blocks'=2,'sec'=8,'pln'=2] {'pln'}, dimensions={0}, use_global_device_ids=true | all-gather | bytes 786432 | tf_op jit(solution)/shard_map/all_gather | solution.py:293
  5.8 0.0 copy-start
  5.8 1.1 %copy-done = bf16[1424,256]{1,0:T(8,128)(2,1)S(1)} copy-done((bf16[1424,256]{1,0:T(8,128)(2,1)S(1)}, bf16[1424,256]{1,0:T(8,128)(2,1)}, u32[]{:S(2)}) %copy-start) | copy-done | bytes 729112
  6.9 0.0 copy-start.1
  6.9 0.9 %copy-done.1 = f32[1,128,512]{2,1,0:T(8,128)S(1)} copy-done((f32[1,128,512]{2,1,0:T(8,128)S(1)}, f32[1,128,512]{2,1,0:T(8,128)}, u32[]{:S(2)}) %copy-start.1) | copy-done | bytes 262168
  7.8 1.2 %shard_map.28.own = f32[3,528,256]{2,1,0:T(8,128)S(1)} custom-call(f32[128,512]{1,0:T(8,128)S(1)} %bitcast.7, f32[2,128,512]{2,1,0:T(8,128)S(1)} %all_gather.9.other, bf16[1424,256]{1,0:T(8,128)(2,1)S(1)} %copy-done), custom_call_target="tpu_custom_call" | custom-call | tf_op jit(solution)/shard_map/pallas_call | solution.py:283
  9.0 0.0 collective-permute-done.1.mine.earlier
  9.0 3.8 %all-gather = f32[256,512]{1,0:T(8,128)S(1)} all-gather(f32[128,512]{1,0:T(8,128)S(1)} %collective-permute-done.1.mine.earlier), channel_id=2, replica_groups=mesh['blocks'=2,'sec'=8,'pln'=2] {'pln'}, dimensions={0}, use_global_device_ids=true | all-gather | bytes 786432 | tf_op jit(solution)/shard_map/all_gather | solution.py:295
  12.8 1.6 %shard_map.29.first = f32[2,32,8,128]{3,2,1,0:T(8,128)S(1)} custom-call(f32[128,512]{1,0:T(8,128)S(1)} %collective-permute-done.1.mine.earlier, f32[2,128,512]{2,1,0:T(8,128)S(1)} %bitcast.3, f32[3,528,256]{2,1,0:T(8,128)S(1)} %shard_map.28.own, bf16[1424,256]{1,0:T(8,128)(2,1)S(1)} %copy-done), custom_call_target="tpu_custom_call" | custom-call | tf_op jit(solution)/shard_map/pallas_call | solution.py:283
  14.4 0.0 collective-permute-done.mine
  14.4 0.4 %collective-permute-start.2 = (f32[128,512]{1,0:T(8,128)S(1)}, f32[128,512]{1,0:T(8,128)S(1)}, u32[]{:S(2)}, u32[]{:S(2)}) collective-permute-start(f32[128,512]{1,0:T(8,128)S(1)} %collective-permute-done.mine), channel_id=1, source_target_pairs={{0,1},{1,0},{2,3},{3,2},{4,5},{5,4},{6,7},{7,6},{8,9},{9,8},{10,11... | collective-permute-start | bytes 786440 | tf_op jit(solution)/shard_map/ppermute | solution.py:262
  14.8 1.6 %shard_map.30 = (f32[32,8,128]{2,1,0:T(8,128)S(1)}, f32[32,8,128]{2,1,0:T(8,128)S(1)}) custom-call(f32[128,512]{1,0:T(8,128)S(1)} %collective-permute-done.mine, f32[128,512]{1,0:T(8,128)S(1)} %collective-permute-done.1.mine.earlier, f32[2,128,512]{2,1,0:T(8,128)S(1)} %bitcast.4, f32[3,528,256]{2,1,0:T(8,128)S(1)} %shard_map.28.own, ...), custom_call_target="tpu_custom_call" | custom-call | tf_op jit(solution)/shard_map/pallas_call | solution.py:283
  16.5 0.0 collective-permute-done.2.other
  16.5 2.4 %shard_map.31 = f32[2,8,4096]{2,1,0:T(8,128)} custom-call(f32[128,512]{1,0:T(8,128)S(1)} %collective-permute-done.mine, f32[128,512]{1,0:T(8,128)S(1)} %collective-permute-done.2.other, f32[3,528,256]{2,1,0:T(8,128)S(1)} %shard_map.28.own, f32[2,32,8,128]{3,2,1,0:T(8,128)S(1)} %shard_map.29.first, f32[32,8,128]{2,1,0:T(8,128)S(1)} %get-tuple-element.15.outer, ...), custom_call_target="tpu_custom_call" | custom-call | tf_op jit(solution)/shard_map/pallas_call | solution.py:283
Async XLA Ops:
  0.0 9.0 %collective-permute-start.1 = (f32[128,512]{1,0:T(8,128)}, f32[128,512]{1,0:T(8,128)S(1)}, u32[]{:S(2)}, u32[]{:S(2)}) collective-permute-start(f32[128,512]{1,0:T(8,128)} %bitcast.5), channel_id=1, source_target_pairs={{0,2},{2,4},{4,6},{6,8},{8,10},{10,12},{12,14},{14,0},{1,3},{3,5},... | collective-permute-start | bytes 786440 | tf_op jit(solution)/shard_map/ppermute | solution.py:258
  1.2 13.2 %collective-permute-start = (f32[128,512]{1,0:T(8,128)}, f32[128,512]{1,0:T(8,128)S(1)}, u32[]{:S(2)}, u32[]{:S(2)}) collective-permute-start(f32[128,512]{1,0:T(8,128)} %bitcast.6), channel_id=1, source_target_pairs={{0,4},{2,6},{4,8},{6,10},{8,12},{10,14},{12,0},{14,2},{1,5},{3,7},... | collective-permute-start | bytes 786440 | tf_op jit(solution)/shard_map/ppermute | solution.py:258
  5.8 1.1 %copy-start = (bf16[1424,256]{1,0:T(8,128)(2,1)S(1)}, bf16[1424,256]{1,0:T(8,128)(2,1)}, u32[]{:S(2)}) copy-start(bf16[1424,256]{1,0:T(8,128)(2,1)} %constant.2.clone.table) | copy-start | bytes 2187268
  6.9 0.9 %copy-start.1 = (f32[1,128,512]{2,1,0:T(8,128)S(1)}, f32[1,128,512]{2,1,0:T(8,128)}, u32[]{:S(2)}) copy-start(f32[1,128,512]{2,1,0:T(8,128)} %param.2) | copy-start | bytes 786436
  14.4 2.1 %collective-permute-start.2 = (f32[128,512]{1,0:T(8,128)S(1)}, f32[128,512]{1,0:T(8,128)S(1)}, u32[]{:S(2)}, u32[]{:S(2)}) collective-permute-start(f32[128,512]{1,0:T(8,128)S(1)} %collective-permute-done.mine), channel_id=1, source_target_pairs={{0,1},{1,0},{2,3},{3,2},{4,5},{5,4},{6,7},{7,6},{8,9},{9,8},{10,11... | collective-permute-start | bytes 786440 | tf_op jit(solution)/shard_map/ppermute | solution.py:262

commit v5 on v4

--- a/solution.py
+++ b/solution.py
@@ -184,17 +184,13 @@
 def first_kernel(at, mine, both, own, table, out, *scratch):
     pln = lax.axis_index("pln")
 
-    def work(present):
-        if not present:
-            out[...] = jnp.zeros_like(out)
-            return
+    @pl.when(lax.rem(lax.axis_index("sec"), 2) == 1)
+    def _():
         here, there = mine[...], both[1 - pln]
         pixels = [outer_row(here, pln == 1)] + inner_rows(here, there, pln == 1)[:1]
         found = surfaces(pixels, lambda r: own[r], *(table.at[x] for x in at), *scratch)
         for r in range(len(pixels)):
             out[r] = found(r)
-
-    reached(1, work)
 
 
 def joined_row(one, two):
@@ -206,26 +202,45 @@
     return (2.0 * joined + before + after) * (1.0 / 16.0)
 
 
-def outer_kernel(at, mine, earlier, both, own, first, table, out, far, *scratch):
+def outer_kernel(at, mine, earlier, both, own, first, table, out, near, far, *scratch):
     pln, sec = lax.axis_index("pln"), lax.axis_index("sec")
-
-    def work(present):
-        parts = [table.at[x] for x in at]
-        beyond = inner_rows(earlier[...], both[1 - pln], pln == 1)[1]
+    odd = lax.rem(sec, 2) == 1
+
+    def found(two, one):
+        outer = [outer_row(mine[...], pln == 1)] if two else []
+        ahead = [outer_row(earlier[...], pln == 1)] + inner_rows(earlier[...], both[1 - pln], pln == 1)
+        rows = ([0] if two else []) + one
+        return surfaces(outer + [ahead[r] for r in one], lambda r: own[rows[r]], *[table.at[x] for x in at], *scratch)
+
+    @pl.when(odd & (sec >= 2))
+    def _():
+        got = found(True, [2])
+        out[...] = joined_row(first[0], got(0))
+        near[...] = first[1]
+        far[...] = got(1)
+
+    @pl.when(jnp.logical_not(odd) & (sec >= 2))
+    def _():
+        got = found(True, [0, 1, 2])
+        two = got(0)
+        out[...] = joined_row(got(1), two)
+        near[...] = got(2)
+        far[...] = got(3)
+
+    @pl.when(sec == 1)
+    def _():
         one = first[0]
-        if present:
-            got = surfaces([outer_row(mine[...], pln == 1), beyond], lambda r: own[2 * r], *parts, *scratch)
-            out[...] = joined_row(one, got(0))
-            far[...] = got(1)
-        else:
-            got = surfaces([beyond], lambda r: own[2], *parts, *scratch)
-            out[...] = joined_row(one, jnp.zeros_like(one))
-            far[...] = jnp.where(sec >= 1, got(0), 0.0)
-
-    reached(2, work)
-
-
-def inner_kernel(at, mine, other, own, first, outer, beyond, table, out, left, spec, half, right, lagged, staged, sent):
+        out[...] = joined_row(one, jnp.zeros_like(one))
+        near[...] = first[1]
+        far[...] = found(False, [2])(0)
+
+    @pl.when(sec == 0)
+    def _():
+        for x in (out, near, far):
+            x[...] = jnp.zeros_like(x)
+
+
+def inner_kernel(at, mine, other, own, outer, beside, beyond, table, out, left, spec, half, right, lagged, staged, sent):
     pln = lax.axis_index("pln")
 
     def send(slot, row, value):
@@ -241,7 +256,7 @@
             pixels = inner_rows(mine[...], other[...], pln == 1)
             parts = (table.at[x] for x in at)
             found = surfaces(pixels, lambda r: own[r + 1], *parts, left, spec, half, right, lagged)
-        near = joined_row(first[1], found(0))
+        near = joined_row(beside[...], found(0))
         ending = outer[...]
         copies = [send(0, pln, 2.0 * ending + near)]
         far = joined_row(beyond[...], found(1))
@@ -296,8 +311,8 @@
     (first,) = call(first_kernel, (2,) + shape, 2, one_back, both, own, table)
     two_back, first = lax.optimization_barrier((two_back, first))
     other = sibling(two_back)
-    outer, beyond = call(outer_kernel, shape, 2, two_back, one_back, both, own, first, table, outs=2)
-    (mixed,) = call(inner_kernel, (2, patches, CROP * CROP), 2, two_back, other, own, first, outer, beyond, table)
+    outer, beside, beyond = call(outer_kernel, shape, 4, two_back, one_back, both, own, first, table, outs=3)
+    (mixed,) = call(inner_kernel, (2, patches, CROP * CROP), 2, two_back, other, own, outer, beside, beyond, table)
     return mixed[None]
 
 

time: 19.1 us -> 18.9 us (0.990)
  the two profiles are of different devices: /device:TPU:13 before, /device:TPU:11 now
where the time goes in v5:
time: 18.9 us; the launch traced here: 18.6 us
  Pallas kernels  6.86 us (36%)
  blocking collectives  5.42 us (29%)
  starting transfers between devices  4.11 us (22%)
  local copies, waits for them, and re-layouts  2.06 us (11%)
    pallas_call x4, Pallas kernels, call(): pl.pallas_call(functools.partial(kernel, at), out_shape=[jax.ShapeDtypeSt...  6.86 us
    all_gather x1, blocking collectives, body(): lax.all_gather(tile, 'pln')  3.24 us
    ppermute x2, starting transfers between devices, from_sections(): return lax.ppermute(tile, 'sec', route)  2.56 us
    all_gather x1, blocking collectives, body(): both = lax.all_gather(one_back, 'pln')  2.18 us
    unnamed x4, local copies, waits for them, and re-layouts  2.06 us
    ppermute x1, starting transfers between devices, sibling(): return lax.ppermute(tile, 'pln', [(0, 1), (1, 0)])  1.55 us
  transfers between devices with their start and end apart: 3, of which 1 were waited for; matrix products, arithmetic and copies ran while one was open for 0% of the time, Pallas kernels for 24%

profile of v5, /device:TPU:11, one launch (start us, length us, event | category | flops | bytes accessed | tf_op | source)
XLA Modules:
  0.0 18.6 jit_solution(17481622420580962581)
XLA Ops:
  0.0 1.3 %collective-permute-start.1 = (f32[128,512]{1,0:T(8,128)}, f32[128,512]{1,0:T(8,128)S(1)}, u32[]{:S(2)}, u32[]{:S(2)}) collective-permute-start(f32[128,512]{1,0:T(8,128)} %bitcast.5), channel_id=1, source_target_pairs={{0,2},{2,4},{4,6},{6,8},{8,10},{10,12},{12,14},{14,0},{1,3},{3,5},... | collective-permute-start | bytes 786440 | tf_op jit(solution)/shard_map/ppermute | solution.py:273
  1.3 1.3 %collective-permute-start = (f32[128,512]{1,0:T(8,128)}, f32[128,512]{1,0:T(8,128)S(1)}, u32[]{:S(2)}, u32[]{:S(2)}) collective-permute-start(f32[128,512]{1,0:T(8,128)} %bitcast.6), channel_id=1, source_target_pairs={{0,4},{2,6},{4,8},{6,10},{8,12},{10,14},{12,0},{14,2},{1,5},{3,7},... | collective-permute-start | bytes 786440 | tf_op jit(solution)/shard_map/ppermute | solution.py:273
  2.6 3.2 %all_gather.9.other = f32[2,128,512]{2,1,0:T(8,128)S(1)} all-gather(f32[1,128,512]{2,1,0:T(8,128)} %param.2), channel_id=1, replica_groups=mesh['blocks'=2,'sec'=8,'pln'=2] {'pln'}, dimensions={0}, use_global_device_ids=true | all-gather | bytes 786432 | tf_op jit(solution)/shard_map/all_gather | solution.py:308
  5.8 0.0 copy-start
  5.8 1.1 %copy-done = bf16[1424,256]{1,0:T(8,128)(2,1)S(1)} copy-done((bf16[1424,256]{1,0:T(8,128)(2,1)S(1)}, bf16[1424,256]{1,0:T(8,128)(2,1)}, u32[]{:S(2)}) %copy-start) | copy-done | bytes 729112
  6.9 0.0 copy-start.1
  6.9 0.9 %copy-done.1 = f32[1,128,512]{2,1,0:T(8,128)S(1)} copy-done((f32[1,128,512]{2,1,0:T(8,128)S(1)}, f32[1,128,512]{2,1,0:T(8,128)}, u32[]{:S(2)}) %copy-start.1) | copy-done | bytes 262168
  7.9 1.2 %shard_map.28.own = f32[3,528,256]{2,1,0:T(8,128)S(1)} custom-call(f32[128,512]{1,0:T(8,128)S(1)} %bitcast.7, f32[2,128,512]{2,1,0:T(8,128)S(1)} %all_gather.9.other, bf16[1424,256]{1,0:T(8,128)(2,1)S(1)} %copy-done), custom_call_target="tpu_custom_call" | custom-call | tf_op jit(solution)/shard_map/pallas_call | solution.py:298
  9.1 0.0 collective-permute-done.1.mine.earlier
  9.1 2.2 %all-gather = f32[256,512]{1,0:T(8,128)S(1)} all-gather(f32[128,512]{1,0:T(8,128)S(1)} %collective-permute-done.1.mine.earlier), channel_id=2, replica_groups=mesh['blocks'=2,'sec'=8,'pln'=2] {'pln'}, dimensions={0}, use_global_device_ids=true | all-gather | bytes 786432 | tf_op jit(solution)/shard_map/all_gather | solution.py:310
  11.3 1.6 %shard_map.29.first = f32[2,32,8,128]{3,2,1,0:T(8,128)S(1)} custom-call(f32[128,512]{1,0:T(8,128)S(1)} %collective-permute-done.1.mine.earlier, f32[2,128,512]{2,1,0:T(8,128)S(1)} %bitcast.3, f32[3,528,256]{2,1,0:T(8,128)S(1)} %shard_map.28.own, bf16[1424,256]{1,0:T(8,128)(2,1)S(1)} %copy-done), custom_call_target="tpu_custom_call" | custom-call | tf_op jit(solution)/shard_map/pallas_call | solution.py:298
  12.8 0.1 collective-permute-done.mine
  13.0 1.5 %collective-permute-start.2 = (f32[128,512]{1,0:T(8,128)S(1)}, f32[128,512]{1,0:T(8,128)S(1)}, u32[]{:S(2)}, u32[]{:S(2)}) collective-permute-start(f32[128,512]{1,0:T(8,128)S(1)} %collective-permute-done.mine), channel_id=1, source_target_pairs={{0,1},{1,0},{2,3},{3,2},{4,5},{5,4},{6,7},{7,6},{8,9},{9,8},{10,11... | collective-permute-start | bytes 786440 | tf_op jit(solution)/shard_map/ppermute | solution.py:277
  14.5 1.7 %shard_map.30 = (f32[32,8,128]{2,1,0:T(8,128)S(1)}, f32[32,8,128]{2,1,0:T(8,128)S(1)}, f32[32,8,128]{2,1,0:T(8,128)S(1)}) custom-call(f32[128,512]{1,0:T(8,128)S(1)} %collective-permute-done.mine, f32[128,512]{1,0:T(8,128)S(1)} %collective-permute-done.1.mine.earlier, f32[2,128,512]{2,1,0:T(8,128)S(1)} %bitcast.4, f32[3,528,256]{2,1,0:T(8,128)S(1)} %shard_map.28.own, ...), custom_call_target="tpu_custom_call" | custom-call | tf_op jit(solution)/shard_map/pallas_call | solution.py:298
  16.2 0.0 collective-permute-done.2.other
  16.2 2.4 %shard_map.31 = f32[2,8,4096]{2,1,0:T(8,128)} custom-call(f32[128,512]{1,0:T(8,128)S(1)} %collective-permute-done.mine, f32[128,512]{1,0:T(8,128)S(1)} %collective-permute-done.2.other, f32[3,528,256]{2,1,0:T(8,128)S(1)} %shard_map.28.own, f32[32,8,128]{2,1,0:T(8,128)S(1)} %get-tuple-element.16.outer, f32[32,8,128]{2,1,0:T(8,128)S(1)} %get-tuple-element.17.beside, ...), custom_call_target="tpu_custom_call" | custom-call | tf_op jit(solution)/shard_map/pallas_call | solution.py:298
Async XLA Ops:
  0.0 9.1 %collective-permute-start.1 = (f32[128,512]{1,0:T(8,128)}, f32[128,512]{1,0:T(8,128)S(1)}, u32[]{:S(2)}, u32[]{:S(2)}) collective-permute-start(f32[128,512]{1,0:T(8,128)} %bitcast.5), channel_id=1, source_target_pairs={{0,2},{2,4},{4,6},{6,8},{8,10},{10,12},{12,14},{14,0},{1,3},{3,5},... | collective-permute-start | bytes 786440 | tf_op jit(solution)/shard_map/ppermute | solution.py:273
  1.3 11.7 %collective-permute-start = (f32[128,512]{1,0:T(8,128)}, f32[128,512]{1,0:T(8,128)S(1)}, u32[]{:S(2)}, u32[]{:S(2)}) collective-permute-start(f32[128,512]{1,0:T(8,128)} %bitcast.6), channel_id=1, source_target_pairs={{0,4},{2,6},{4,8},{6,10},{8,12},{10,14},{12,0},{14,2},{1,5},{3,7},... | collective-permute-start | bytes 786440 | tf_op jit(solution)/shard_map/ppermute | solution.py:273
  5.8 1.1 %copy-start = (bf16[1424,256]{1,0:T(8,128)(2,1)S(1)}, bf16[1424,256]{1,0:T(8,128)(2,1)}, u32[]{:S(2)}) copy-start(bf16[1424,256]{1,0:T(8,128)(2,1)} %constant.2.clone.table) | copy-start | bytes 2187268
  6.9 0.9 %copy-start.1 = (f32[1,128,512]{2,1,0:T(8,128)S(1)}, f32[1,128,512]{2,1,0:T(8,128)}, u32[]{:S(2)}) copy-start(f32[1,128,512]{2,1,0:T(8,128)} %param.2) | copy-start | bytes 786436
  13.0 3.2 %collective-permute-start.2 = (f32[128,512]{1,0:T(8,128)S(1)}, f32[128,512]{1,0:T(8,128)S(1)}, u32[]{:S(2)}, u32[]{:S(2)}) collective-permute-start(f32[128,512]{1,0:T(8,128)S(1)} %collective-permute-done.mine), channel_id=1, source_target_pairs={{0,1},{1,0},{2,3},{3,2},{4,5},{5,4},{6,7},{7,6},{8,9},{9,8},{10,11... | collective-permute-start | bytes 786440 | tf_op jit(solution)/shard_map/ppermute | solution.py:277

commit v6 on v5

--- a/solution.py
+++ b/solution.py
@@ -187,7 +187,7 @@
     @pl.when(lax.rem(lax.axis_index("sec"), 2) == 1)
     def _():
         here, there = mine[...], both[1 - pln]
-        pixels = [outer_row(here, pln == 1)] + inner_rows(here, there, pln == 1)[:1]
+        pixels = [outer_row(here, pln == 1)] + inner_rows(here, there, pln == 1)
         found = surfaces(pixels, lambda r: own[r], *(table.at[x] for x in at), *scratch)
         for r in range(len(pixels)):
             out[r] = found(r)
@@ -214,10 +214,9 @@
 
     @pl.when(odd & (sec >= 2))
     def _():
-        got = found(True, [2])
-        out[...] = joined_row(first[0], got(0))
+        out[...] = joined_row(first[0], found(True, [])(0))
         near[...] = first[1]
-        far[...] = got(1)
+        far[...] = first[2]
 
     @pl.when(jnp.logical_not(odd) & (sec >= 2))
     def _():
@@ -232,7 +231,7 @@
         one = first[0]
         out[...] = joined_row(one, jnp.zeros_like(one))
         near[...] = first[1]
-        far[...] = found(False, [2])(0)
+        far[...] = first[2]
 
     @pl.when(sec == 0)
     def _():
@@ -308,7 +307,7 @@
     (own,) = call(own_kernel, (3, packed, 2 * PATCH), 3, tile, lax.all_gather(tile, "pln"), table)
     one_back, own = lax.optimization_barrier((one_back, own))
     both = lax.all_gather(one_back, "pln")
-    (first,) = call(first_kernel, (2,) + shape, 2, one_back, both, own, table)
+    (first,) = call(first_kernel, (3,) + shape, 3, one_back, both, own, table)
     two_back, first = lax.optimization_barrier((two_back, first))
     other = sibling(two_back)
     outer, beside, beyond = call(outer_kernel, shape, 4, two_back, one_back, both, own, first, table, outs=3)

time: 18.9 us -> 18.6 us (0.984)
  starting transfers between devices: 4.11 us -> 3.71 us
  Pallas kernels: 6.86 us -> 7.18 us
    ppermute x1, starting transfers between devices: 1.55 us -> 1.15 us  [sibling(): return lax.ppermute(tile, 'pln', [(0, 1), (1, 0)])]
    pallas_call x4, Pallas kernels: 6.86 us -> 7.18 us  [call(): pl.pallas_call(functools.partial(kernel, at), out_shape=[jax.ShapeDtypeSt...]
  transfers between devices with their start and end apart: 3 -> 3, of which waited for: 1 -> 0; matrix products, arithmetic and copies ran while one was open for 0% -> 0% of each run, Pallas kernels for 24% -> 26%
where the time goes in v6:
time: 18.6 us; the launch traced here: 18.4 us
  Pallas kernels  7.18 us (39%)
  blocking collectives  5.42 us (29%)
  starting transfers between devices  3.71 us (20%)
  local copies, waits for them, and re-layouts  2.06 us (11%)
    pallas_call x4, Pallas kernels, call(): pl.pallas_call(functools.partial(kernel, at), out_shape=[jax.ShapeDtypeSt...  7.18 us
    all_gather x1, blocking collectives, body(): lax.all_gather(tile, 'pln')  3.24 us
    ppermute x2, starting transfers between devices, from_sections(): return lax.ppermute(tile, 'sec', route)  2.56 us
    all_gather x1, blocking collectives, body(): both = lax.all_gather(one_back, 'pln')  2.18 us
    unnamed x4, local copies, waits for them, and re-layouts  2.06 us
    ppermute x1, starting transfers between devices, sibling(): return lax.ppermute(tile, 'pln', [(0, 1), (1, 0)])  1.15 us
  transfers between devices with their start and end apart: 3, of which 0 were waited for; matrix products, arithmetic and copies ran while one was open for 0% of the time, Pallas kernels for 26%

profile of v6, /device:TPU:11, one launch (start us, length us, event | category | flops | bytes accessed | tf_op | source)
XLA Modules:
  0.0 18.4 jit_solution(73292591797496088)
XLA Ops:
  0.0 1.3 %collective-permute-start.1 = (f32[128,512]{1,0:T(8,128)}, f32[128,512]{1,0:T(8,128)S(1)}, u32[]{:S(2)}, u32[]{:S(2)}) collective-permute-start(f32[128,512]{1,0:T(8,128)} %bitcast.5), channel_id=1, source_target_pairs={{0,2},{2,4},{4,6},{6,8},{8,10},{10,12},{12,14},{14,0},{1,3},{3,5},... | collective-permute-start | bytes 786440 | tf_op jit(solution)/shard_map/ppermute | solution.py:272
  1.3 1.3 %collective-permute-start = (f32[128,512]{1,0:T(8,128)}, f32[128,512]{1,0:T(8,128)S(1)}, u32[]{:S(2)}, u32[]{:S(2)}) collective-permute-start(f32[128,512]{1,0:T(8,128)} %bitcast.6), channel_id=1, source_target_pairs={{0,4},{2,6},{4,8},{6,10},{8,12},{10,14},{12,0},{14,2},{1,5},{3,7},... | collective-permute-start | bytes 786440 | tf_op jit(solution)/shard_map/ppermute | solution.py:272
  2.6 3.2 %all_gather.9.other = f32[2,128,512]{2,1,0:T(8,128)S(1)} all-gather(f32[1,128,512]{2,1,0:T(8,128)} %param.2), channel_id=1, replica_groups=mesh['blocks'=2,'sec'=8,'pln'=2] {'pln'}, dimensions={0}, use_global_device_ids=true | all-gather | bytes 786432 | tf_op jit(solution)/shard_map/all_gather | solution.py:307
  5.8 0.0 copy-start
  5.8 1.1 %copy-done = bf16[1424,256]{1,0:T(8,128)(2,1)S(1)} copy-done((bf16[1424,256]{1,0:T(8,128)(2,1)S(1)}, bf16[1424,256]{1,0:T(8,128)(2,1)}, u32[]{:S(2)}) %copy-start) | copy-done | bytes 729112
  6.9 0.0 copy-start.1
  6.9 0.9 %copy-done.1 = f32[1,128,512]{2,1,0:T(8,128)S(1)} copy-done((f32[1,128,512]{2,1,0:T(8,128)S(1)}, f32[1,128,512]{2,1,0:T(8,128)}, u32[]{:S(2)}) %copy-start.1) | copy-done | bytes 262168
  7.9 1.2 %shard_map.28.own = f32[3,528,256]{2,1,0:T(8,128)S(1)} custom-call(f32[128,512]{1,0:T(8,128)S(1)} %bitcast.7, f32[2,128,512]{2,1,0:T(8,128)S(1)} %all_gather.9.other, bf16[1424,256]{1,0:T(8,128)(2,1)S(1)} %copy-done), custom_call_target="tpu_custom_call" | custom-call | tf_op jit(solution)/shard_map/pallas_call | solution.py:297
  9.1 0.0 collective-permute-done.1.mine.earlier
  9.1 2.2 %all-gather = f32[256,512]{1,0:T(8,128)S(1)} all-gather(f32[128,512]{1,0:T(8,128)S(1)} %collective-permute-done.1.mine.earlier), channel_id=2, replica_groups=mesh['blocks'=2,'sec'=8,'pln'=2] {'pln'}, dimensions={0}, use_global_device_ids=true | all-gather | bytes 786432 | tf_op jit(solution)/shard_map/all_gather | solution.py:309
  11.3 2.1 %shard_map.29.first = f32[3,32,8,128]{3,2,1,0:T(8,128)S(1)} custom-call(f32[128,512]{1,0:T(8,128)S(1)} %collective-permute-done.1.mine.earlier, f32[2,128,512]{2,1,0:T(8,128)S(1)} %bitcast.3, f32[3,528,256]{2,1,0:T(8,128)S(1)} %shard_map.28.own, bf16[1424,256]{1,0:T(8,128)(2,1)S(1)} %copy-done), custom_call_target="tpu_custom_call" | custom-call | tf_op jit(solution)/shard_map/pallas_call | solution.py:297
  13.4 0.0 collective-permute-done.mine
  13.4 1.1 %collective-permute-start.2 = (f32[128,512]{1,0:T(8,128)S(1)}, f32[128,512]{1,0:T(8,128)S(1)}, u32[]{:S(2)}, u32[]{:S(2)}) collective-permute-start(f32[128,512]{1,0:T(8,128)S(1)} %collective-permute-done.mine), channel_id=1, source_target_pairs={{0,1},{1,0},{2,3},{3,2},{4,5},{5,4},{6,7},{7,6},{8,9},{9,8},{10,11... | collective-permute-start | bytes 786440 | tf_op jit(solution)/shard_map/ppermute | solution.py:276
  14.5 1.5 %shard_map.30 = (f32[32,8,128]{2,1,0:T(8,128)S(1)}, f32[32,8,128]{2,1,0:T(8,128)S(1)}, f32[32,8,128]{2,1,0:T(8,128)S(1)}) custom-call(f32[128,512]{1,0:T(8,128)S(1)} %collective-permute-done.mine, f32[128,512]{1,0:T(8,128)S(1)} %collective-permute-done.1.mine.earlier, f32[2,128,512]{2,1,0:T(8,128)S(1)} %bitcast.4, f32[3,528,256]{2,1,0:T(8,128)S(1)} %shard_map.28.own, ...), custom_call_target="tpu_custom_call" | custom-call | tf_op jit(solution)/shard_map/pallas_call | solution.py:297
  16.0 0.0 collective-permute-done.2.other
  16.0 2.4 %shard_map.31 = f32[2,8,4096]{2,1,0:T(8,128)} custom-call(f32[128,512]{1,0:T(8,128)S(1)} %collective-permute-done.mine, f32[128,512]{1,0:T(8,128)S(1)} %collective-permute-done.2.other, f32[3,528,256]{2,1,0:T(8,128)S(1)} %shard_map.28.own, f32[32,8,128]{2,1,0:T(8,128)S(1)} %get-tuple-element.16.outer, f32[32,8,128]{2,1,0:T(8,128)S(1)} %get-tuple-element.17.beside, ...), custom_call_target="tpu_custom_call" | custom-call | tf_op jit(solution)/shard_map/pallas_call | solution.py:297
Async XLA Ops:
  0.0 9.1 %collective-permute-start.1 = (f32[128,512]{1,0:T(8,128)}, f32[128,512]{1,0:T(8,128)S(1)}, u32[]{:S(2)}, u32[]{:S(2)}) collective-permute-start(f32[128,512]{1,0:T(8,128)} %bitcast.5), channel_id=1, source_target_pairs={{0,2},{2,4},{4,6},{6,8},{8,10},{10,12},{12,14},{14,0},{1,3},{3,5},... | collective-permute-start | bytes 786440 | tf_op jit(solution)/shard_map/ppermute | solution.py:272
  1.3 12.1 %collective-permute-start = (f32[128,512]{1,0:T(8,128)}, f32[128,512]{1,0:T(8,128)S(1)}, u32[]{:S(2)}, u32[]{:S(2)}) collective-permute-start(f32[128,512]{1,0:T(8,128)} %bitcast.6), channel_id=1, source_target_pairs={{0,4},{2,6},{4,8},{6,10},{8,12},{10,14},{12,0},{14,2},{1,5},{3,7},... | collective-permute-start | bytes 786440 | tf_op jit(solution)/shard_map/ppermute | solution.py:272
  5.8 1.1 %copy-start = (bf16[1424,256]{1,0:T(8,128)(2,1)S(1)}, bf16[1424,256]{1,0:T(8,128)(2,1)}, u32[]{:S(2)}) copy-start(bf16[1424,256]{1,0:T(8,128)(2,1)} %constant.2.clone.table) | copy-start | bytes 2187268
  6.9 0.9 %copy-start.1 = (f32[1,128,512]{2,1,0:T(8,128)S(1)}, f32[1,128,512]{2,1,0:T(8,128)}, u32[]{:S(2)}) copy-start(f32[1,128,512]{2,1,0:T(8,128)} %param.2) | copy-start | bytes 786436
  13.4 2.6 %collective-permute-start.2 = (f32[128,512]{1,0:T(8,128)S(1)}, f32[128,512]{1,0:T(8,128)S(1)}, u32[]{:S(2)}, u32[]{:S(2)}) collective-permute-start(f32[128,512]{1,0:T(8,128)S(1)} %collective-permute-done.mine), channel_id=1, source_target_pairs={{0,1},{1,0},{2,3},{3,2},{4,5},{5,4},{6,7},{7,6},{8,9},{9,8},{10,11... | collective-permute-start | bytes 786440 | tf_op jit(solution)/shard_map/ppermute | solution.py:276
